TPU v7x, 32 devices: a whole 2x2x4 slice. The times are simulated.
32 devices in a mesh: seq: 8 (over y, x, core), fsdp: 4 (over z).
Axes of the slice: x: 2, y: 2, z: 4, core: 2. Of those that a mesh axis runs over, the one named last changes fastest.
Arguments:
- tokens: bfloat16 [8, 4096, 640], P('fsdp', 'seq'), may hold values from -6 to 6
- doc_starts: int32 [8, 4096], P('fsdp', 'seq'), may hold values from 0 to 1, as said below
- w_query: bfloat16 [640, 1024], P('fsdp'), may hold values from -0.25 to 0.25
- w_key: bfloat16 [640, 256], P('fsdp'), may hold values from -0.25 to 0.25
- w_value: bfloat16 [640, 256], P('fsdp'), may hold values from -0.25 to 0.25
- w_out: bfloat16 [1024, 640], P('fsdp'), may hold values from -1.5 to 1.5
- w_gate: bfloat16 [640, 2048], P('fsdp'), may hold values from -0.25 to 0.25
- w_up: bfloat16 [640, 2048], P('fsdp'), may hold values from -0.25 to 0.25
- w_down: bfloat16 [2048, 640], P('fsdp'), may hold values from -0.125 to 0.125
- pre_attn: float32 [640], replicated, may hold values from 0.25 to 1.75
- post_attn: float32 [640], replicated, may hold values from 0.25 to 1.75
- pre_ffn: float32 [640], replicated, may hold values from 0.25 to 1.75
- post_ffn: float32 [640], replicated, may hold values from 0.25 to 1.75
- query_norm: float32 [256], replicated, may hold values from 0.25 to 1.75
- key_norm: float32 [256], replicated, may hold values from 0.25 to 1.75
- cotangent: bfloat16 [8, 4096, 640], P('fsdp', 'seq'), may hold values from -6 to 6
Outputs:
- layer_out: bfloat16 [8, 4096, 640], P('fsdp', 'seq')
- dtokens: bfloat16 [8, 4096, 640], P('fsdp', 'seq')
- dw_query: float32 [640, 1024], P('fsdp', 'seq')
- dw_key: float32 [640, 256], P('fsdp', 'seq')
- dw_value: float32 [640, 256], P('fsdp', 'seq')
- dw_out: float32 [1024, 640], P('fsdp', 'seq')
- dw_gate: float32 [640, 2048], P('fsdp', 'seq')
- dw_up: float32 [640, 2048], P('fsdp', 'seq')
- dw_down: float32 [2048, 640], P('fsdp', 'seq')
- dpre_attn: float32 [640], replicated
- dpost_attn: float32 [640], replicated
- dpre_ffn: float32 [640], replicated
- dpost_ffn: float32 [640], replicated
- dquery_norm: float32 [256], replicated
- dkey_norm: float32 [256], replicated
Inputs may be any that keep to these rules, and one draw needn't show every extreme that they name: `doc_starts`: 1 marks the first token of a document, 0 any other token; the first token of every sequence is 1.
All inputs are finite; a program needn't handle non-finite values.
Results may differ from a plain program's by a relative error of at most 0.022.
Values may be sent and summed in bfloat16 or wider, within the bound.
No kernel may reach another device: no remote copies, remote signals or barrier semaphores. Data moves between devices by JAX's collectives and lax.ppermute only.
A program may use at most 192 MiB of HBM per device.

v0:
```python
import jax
import jax.numpy as jnp
from jax import lax
from jax.sharding import PartitionSpec as P

WINDOW = 512


epsilon = 1e-06
NEG_FILL = -1e30
ROPE_BASE = 10000.0


def carried_in(value, axis, join, neutral):
    count, mine = (lax.axis_size(axis), lax.axis_index(axis))
    pieces = lax.all_gather(value, axis)
    subtotal = jnp.full_like(value, 0) + jnp.asarray(neutral, value.dtype)

    def step(position, subtotal):
        longer = join(subtotal, pieces[position])
        return jnp.where(position < mine, longer, subtotal)

    return lax.fori_loop(0, count - 1, step, subtotal)


def passed_along(shard, axis, by):
    length = lax.axis_size(axis)
    pairs = [(i, i + by) for i in range(length) if 0 <= i + by < length]
    return lax.ppermute(shard, axis, pairs)


def norm_rows(vector, gain_vec):
    return (
        vector * lax.rsqrt(jnp.mean(vector * vector, axis=-1, keepdims=True) + epsilon) * gain_vec
    )


def rotate(vector, cosine, sine_tab):
    half_width = vector.shape[-1] // 2
    first_half = vector[..., :half_width]
    second_half = vector[..., half_width:]
    turned = jnp.concatenate([-second_half, first_half], axis=-1)
    return vector * cosine + turned * sine_tab


def tables(positions, head_dim):
    half_width = head_dim // 2
    frequency = ROPE_BASE ** (-(jnp.arange(half_width, dtype=jnp.float32) * 2.0) / head_dim)
    angles = positions.astype(jnp.float32)[..., None] * frequency
    angles = jnp.concatenate([angles, angles], axis=-1)
    return (jnp.cos(angles), jnp.sin(angles))


def gated_unit(gate_proj, up_proj):
    return jax.nn.gelu(gate_proj, approximate=True) * up_proj


def body(
    tokens,
    doc_starts,
    w_query,
    w_key,
    w_value,
    w_out,
    w_gate,
    w_up,
    w_down,
    pre_attn,
    post_attn,
    pre_ffn,
    post_ffn,
    query_norm,
    key_norm,
    cotangent,
):
    seq_dev, block_len, _ = tokens.shape
    head_dim = w_key.shape[1]
    head_count = w_query.shape[1] // head_dim
    scaling = head_dim ** (-0.5)
    offset = lax.axis_index("seq") * block_len
    indices = offset + jnp.arange(block_len, dtype=jnp.int32)
    marked = jnp.where(doc_starts == 1, indices[None, :], -1)
    before = carried_in(
        jnp.max(marked, axis=1), "seq", jnp.maximum, jnp.full((seq_dev,), -1, jnp.int32)
    )
    latest = jnp.maximum(lax.cummax(marked, axis=1), before[:, None])
    positions = indices[None, :] - latest
    cosine, sine_tab = tables(positions, head_dim)
    reach_hops = -(-(WINDOW - 1) // block_len)
    row_ids = jnp.arange(block_len, dtype=jnp.int32)
    col_ids = jnp.arange((reach_hops + 1) * block_len, dtype=jnp.int32)
    distance = reach_hops * block_len + row_ids[:, None] - col_ids[None, :]
    reach_cap = jnp.minimum(positions, WINDOW - 1)
    allowed = ((distance[None] >= 0) & (distance[None] <= reach_cap[:, :, None]))[:, None]
    tokens_f = tokens.astype(jnp.float32)
    attn_in, pull_attnpre = jax.vjp(norm_rows, tokens_f, pre_attn)
    attn_low = attn_in.astype(jnp.bfloat16)
    full_query, full_key, full_value, full_out = (
        lax.all_gather(w_query, "fsdp", axis=0, tiled=True),
        lax.all_gather(w_key, "fsdp", axis=0, tiled=True),
        lax.all_gather(w_value, "fsdp", axis=0, tiled=True),
        lax.all_gather(w_out, "fsdp", axis=0, tiled=True),
    )
    query_raw = jnp.einsum(
        "sbd,df->sbf", attn_low, full_query, preferred_element_type=jnp.float32
    ).reshape(seq_dev, block_len, head_count, head_dim)
    key_raw = jnp.einsum("sbd,df->sbf", attn_low, full_key, preferred_element_type=jnp.float32)
    value_raw = jnp.einsum("sbd,df->sbf", attn_low, full_value, preferred_element_type=jnp.float32)
    query_rot, pull_query = jax.vjp(
        lambda raw_part, gain_part: rotate(
            norm_rows(raw_part, gain_part), cosine[:, :, None, :], sine_tab[:, :, None, :]
        ),
        query_raw,
        query_norm,
    )
    key_rot, pull_key = jax.vjp(
        lambda raw_part, gain_part: rotate(norm_rows(raw_part, gain_part), cosine, sine_tab),
        key_raw,
        key_norm,
    )
    query_low = query_rot.astype(jnp.bfloat16)
    key_low = key_rot.astype(jnp.bfloat16)
    value_low = value_raw.astype(jnp.bfloat16)
    key_parts = [key_low]
    value_parts = [value_low]
    hop_index = 1
    far_key, far_value = passed_along((key_low, value_low), "seq", hop_index)
    key_parts.insert(0, far_key)
    value_parts.insert(0, far_value)
    key_rows = jnp.concatenate(key_parts, axis=1)
    value_rows = jnp.concatenate(value_parts, axis=1)

    def score_block(query_part):
        raw_dot = (
            jnp.einsum("sqhd,skd->shqk", query_part, key_rows, preferred_element_type=jnp.float32)
            * scaling
        )
        return jnp.where(allowed, raw_dot, NEG_FILL)

    scores = score_block(query_low)
    largest = jnp.max(scores, axis=-1, keepdims=True)
    exponent = jnp.exp(scores - largest)
    totals = jnp.sum(exponent, axis=-1, keepdims=True)
    probs_full = exponent / totals
    log_total = largest + jnp.log(totals)
    context = jnp.einsum(
        "shqk,skd->sqhd",
        probs_full.astype(jnp.bfloat16),
        value_rows,
        preferred_element_type=jnp.float32,
    )
    context_low = context.reshape(seq_dev, block_len, head_count * head_dim).astype(jnp.bfloat16)
    attn_branch = jnp.einsum(
        "sbf,fd->sbd", context_low, full_out, preferred_element_type=jnp.float32
    )
    attn_normed, pull_attnpost = jax.vjp(norm_rows, attn_branch, post_attn)
    residual = tokens_f + attn_normed
    ffn_in, pull_ffnpre = jax.vjp(norm_rows, residual, pre_ffn)
    ffn_low = ffn_in.astype(jnp.bfloat16)
    full_gate, full_up, full_down = (
        lax.all_gather(w_gate, "fsdp", axis=0, tiled=True),
        lax.all_gather(w_up, "fsdp", axis=0, tiled=True),
        lax.all_gather(w_down, "fsdp", axis=0, tiled=True),
    )
    gate_proj = jnp.einsum("sbd,df->sbf", ffn_low, full_gate, preferred_element_type=jnp.float32)
    up_proj = jnp.einsum("sbd,df->sbf", ffn_low, full_up, preferred_element_type=jnp.float32)
    hidden, pull_gated = jax.vjp(gated_unit, gate_proj, up_proj)
    hidden_low = hidden.astype(jnp.bfloat16)
    ffn_branch = jnp.einsum(
        "sbf,fd->sbd", hidden_low, full_down, preferred_element_type=jnp.float32
    )
    ffn_normed, pull_ffnpost = jax.vjp(norm_rows, ffn_branch, post_ffn)
    layer_out = (residual + ffn_normed).astype(jnp.bfloat16)
    cot_full = cotangent.astype(jnp.float32)
    g_ffnbranch, gp_ffnpost = pull_ffnpost(cot_full)
    g_ffnlow = g_ffnbranch.astype(jnp.bfloat16)
    full_gate, full_up, full_down = (
        lax.all_gather(w_gate, "fsdp", axis=0, tiled=True),
        lax.all_gather(w_up, "fsdp", axis=0, tiled=True),
        lax.all_gather(w_down, "fsdp", axis=0, tiled=True),
    )
    g_hidden = jnp.einsum("sbd,fd->sbf", g_ffnlow, full_down, preferred_element_type=jnp.float32)
    part_down = jnp.einsum("sbf,sbd->fd", hidden_low, g_ffnlow, preferred_element_type=jnp.float32)
    g_gate, g_up = pull_gated(g_hidden)
    g_gatelow = g_gate.astype(jnp.bfloat16)
    g_uplow = g_up.astype(jnp.bfloat16)
    g_ffnin = jnp.einsum("sbf,df->sbd", g_gatelow, full_gate, preferred_element_type=jnp.float32)
    g_ffnin = g_ffnin + jnp.einsum(
        "sbf,df->sbd", g_uplow, full_up, preferred_element_type=jnp.float32
    )
    part_gate = jnp.einsum("sbd,sbf->df", ffn_low, g_gatelow, preferred_element_type=jnp.float32)
    part_up = jnp.einsum("sbd,sbf->df", ffn_low, g_uplow, preferred_element_type=jnp.float32)
    g_resnorm, gp_ffnpre = pull_ffnpre(g_ffnin)
    g_residual = cot_full + g_resnorm
    g_attnbranch, gp_attnpost = pull_attnpost(g_residual)
    g_attnlow = g_attnbranch.astype(jnp.bfloat16)
    full_query, full_key, full_value, full_out = (
        lax.all_gather(w_query, "fsdp", axis=0, tiled=True),
        lax.all_gather(w_key, "fsdp", axis=0, tiled=True),
        lax.all_gather(w_value, "fsdp", axis=0, tiled=True),
        lax.all_gather(w_out, "fsdp", axis=0, tiled=True),
    )
    g_context = jnp.einsum("sbd,fd->sbf", g_attnlow, full_out, preferred_element_type=jnp.float32)
    g_context = g_context.astype(jnp.bfloat16).reshape(seq_dev, block_len, head_count, head_dim)
    part_out = jnp.einsum("sbf,sbd->fd", context_low, g_attnlow, preferred_element_type=jnp.float32)
    probs_again = jnp.exp(score_block(query_low) - log_total)
    g_probs = jnp.einsum(
        "sqhd,skd->shqk", g_context, value_rows, preferred_element_type=jnp.float32
    )
    spread = jnp.sum(g_probs * probs_again, axis=-1, keepdims=True)
    g_scores = (probs_again * (g_probs - spread)).astype(jnp.bfloat16)
    g_queryrot = (
        jnp.einsum("shqk,skd->sqhd", g_scores, key_rows, preferred_element_type=jnp.float32)
        * scaling
    )
    g_keys = (
        jnp.einsum("shqk,sqhd->skd", g_scores, query_low, preferred_element_type=jnp.float32)
        * scaling
    )
    g_values = jnp.einsum(
        "shqk,sqhd->skd",
        probs_again.astype(jnp.bfloat16),
        g_context,
        preferred_element_type=jnp.float32,
    )
    g_keyrot = g_keys[:, reach_hops * block_len :]
    g_value = g_values[:, reach_hops * block_len :]
    hop_index = 1
    col_start = (reach_hops - hop_index) * block_len
    near_key = passed_along(
        g_keys[:, col_start : col_start + block_len].astype(jnp.bfloat16), "seq", -hop_index
    ).astype(jnp.float32)
    near_value = passed_along(
        g_values[:, col_start : col_start + block_len].astype(jnp.bfloat16), "seq", -hop_index
    ).astype(jnp.float32)
    g_keyrot = g_keyrot + near_key
    g_value = g_value + near_value
    g_queryraw, gp_query = pull_query(g_queryrot)
    g_keyraw, gp_key = pull_key(g_keyrot)
    g_querylow = g_queryraw.reshape(seq_dev, block_len, head_count * head_dim).astype(jnp.bfloat16)
    g_keylow = g_keyraw.astype(jnp.bfloat16)
    g_valuelow = g_value.astype(jnp.bfloat16)
    g_attnin = jnp.einsum("sbf,df->sbd", g_querylow, full_query, preferred_element_type=jnp.float32)
    g_attnin = g_attnin + jnp.einsum(
        "sbf,df->sbd", g_keylow, full_key, preferred_element_type=jnp.float32
    )
    g_attnin = g_attnin + jnp.einsum(
        "sbf,df->sbd", g_valuelow, full_value, preferred_element_type=jnp.float32
    )
    part_query = jnp.einsum("sbd,sbf->df", attn_low, g_querylow, preferred_element_type=jnp.float32)
    part_key = jnp.einsum("sbd,sbf->df", attn_low, g_keylow, preferred_element_type=jnp.float32)
    part_value = jnp.einsum("sbd,sbf->df", attn_low, g_valuelow, preferred_element_type=jnp.float32)
    g_tokensnorm, gp_attnpre = pull_attnpre(g_attnin)
    dtokens = (g_residual + g_tokensnorm).astype(jnp.bfloat16)
    col_query, col_key, col_value, col_out, col_gate, col_up, col_down = (
        lax.psum_scatter(
            part_query.astype(jnp.bfloat16), "seq", scatter_dimension=1, tiled=True
        ).astype(jnp.float32),
        lax.psum_scatter(
            part_key.astype(jnp.bfloat16), "seq", scatter_dimension=1, tiled=True
        ).astype(jnp.float32),
        lax.psum_scatter(
            part_value.astype(jnp.bfloat16), "seq", scatter_dimension=1, tiled=True
        ).astype(jnp.float32),
        lax.psum_scatter(
            part_out.astype(jnp.bfloat16), "seq", scatter_dimension=1, tiled=True
        ).astype(jnp.float32),
        lax.psum_scatter(
            part_gate.astype(jnp.bfloat16), "seq", scatter_dimension=1, tiled=True
        ).astype(jnp.float32),
        lax.psum_scatter(
            part_up.astype(jnp.bfloat16), "seq", scatter_dimension=1, tiled=True
        ).astype(jnp.float32),
        lax.psum_scatter(
            part_down.astype(jnp.bfloat16), "seq", scatter_dimension=1, tiled=True
        ).astype(jnp.float32),
    )
    dw_query, dw_key, dw_value, dw_out, dw_gate, dw_up, dw_down = (
        lax.psum_scatter(
            col_query.astype(jnp.bfloat16), "fsdp", scatter_dimension=0, tiled=True
        ).astype(jnp.float32),
        lax.psum_scatter(
            col_key.astype(jnp.bfloat16), "fsdp", scatter_dimension=0, tiled=True
        ).astype(jnp.float32),
        lax.psum_scatter(
            col_value.astype(jnp.bfloat16), "fsdp", scatter_dimension=0, tiled=True
        ).astype(jnp.float32),
        lax.psum_scatter(
            col_out.astype(jnp.bfloat16), "fsdp", scatter_dimension=0, tiled=True
        ).astype(jnp.float32),
        lax.psum_scatter(
            col_gate.astype(jnp.bfloat16), "fsdp", scatter_dimension=0, tiled=True
        ).astype(jnp.float32),
        lax.psum_scatter(
            col_up.astype(jnp.bfloat16), "fsdp", scatter_dimension=0, tiled=True
        ).astype(jnp.float32),
        lax.psum_scatter(
            col_down.astype(jnp.bfloat16), "fsdp", scatter_dimension=0, tiled=True
        ).astype(jnp.float32),
    )
    dpre_attn, dpost_attn, dpre_ffn, dpost_ffn, dquery_norm, dkey_norm = lax.psum(
        (gp_attnpre, gp_attnpost, gp_ffnpre, gp_ffnpost, gp_query, gp_key), ("seq", "fsdp")
    )
    return (
        layer_out,
        dtokens,
        dw_query,
        dw_key,
        dw_value,
        dw_out,
        dw_gate,
        dw_up,
        dw_down,
        dpre_attn,
        dpost_attn,
        dpre_ffn,
        dpost_ffn,
        dquery_norm,
        dkey_norm,
    )


def solution(mesh):
    in_specs = (
        P("fsdp", "seq", None),
        P("fsdp", "seq"),
        P("fsdp", None),
        P("fsdp", None),
        P("fsdp", None),
        P("fsdp", None),
        P("fsdp", None),
        P("fsdp", None),
        P("fsdp", None),
        P(),
        P(),
        P(),
        P(),
        P(),
        P(),
        P("fsdp", "seq", None),
    )
    out_specs = (
        P("fsdp", "seq", None),
        P("fsdp", "seq", None),
        P("fsdp", "seq"),
        P("fsdp", "seq"),
        P("fsdp", "seq"),
        P("fsdp", "seq"),
        P("fsdp", "seq"),
        P("fsdp", "seq"),
        P("fsdp", "seq"),
        P(),
        P(),
        P(),
        P(),
        P(),
        P(),
    )
    return jax.shard_map(body, mesh=mesh, in_specs=in_specs, out_specs=out_specs, check_vma=False)
```

profile of v0, /device:TPU:0, one launch (start us, length us, event | category | flops | bytes accessed | tf_op | source)
XLA Modules:
  0.0 768.5 jit_solution(187058222494560108)
XLA Ops:
  11.1 17.9 %all_gather.34 = bf16[640,256]{1,0:T(8,128)(2,1)S(1)} all-gather(bf16[160,256]{1,0:T(8,128)(2,1)S(1)} %copy-done.44), channel_id=1, replica_groups=mesh['seq'=8,'fsdp'=4] {'fsdp'}, dimensions={0}, use_global_device_ids=true | all-gather | bytes 409600 | tf_op jit(solution)/shard_map/all_gather | solution.py:101
  34.3 7.9 %all-reduce.4 = s32[16]{0:T(128)S(1)} all-reduce(s32[16]{0:T(128)S(1)} %dynamic-update-slice), channel_id=2, replica_groups=mesh['seq'=8,'fsdp'=4] {'seq'}, use_global_device_ids=true, to_apply=%add.4 | all-reduce | flops 16 | bytes 128
  43.4 15.8 %all_gather.37 = bf16[640,256]{1,0:T(8,128)(2,1)S(1)} all-gather(bf16[160,256]{1,0:T(8,128)(2,1)S(1)} %copy-done.45), channel_id=1, replica_groups=mesh['seq'=8,'fsdp'=4] {'fsdp'}, dimensions={0}, use_global_device_ids=true | all-gather | bytes 409600 | tf_op jit(solution)/shard_map/all_gather | solution.py:100
  98.9 9.1 %fusion.107 = (f32[2,4,512]{2,1,0:T(4,128)S(1)}, f32[2,4,512,1024]{2,3,1,0:T(8,128)}) fusion(bf16[2,512,4,256]{1,3,2,0:T(8,128)(2,1)S(1)} %fusion.18, bf16[2,512,256]{1,2,0:T(8,128)(2,1)} %get-tuple-element.159, bf16[2,512,256]{1,2,0:T(8,128)(2,1)S(1)} %collective-permute-done.1, pred[2,512,1024]{1,2,0:T(8,128)(4,1)S(1)} %copy-done.33), kind=kOutput, calls=%fused_computation.188 | convolution fusion | flops 2162159616 | bytes 20987904 | tf_op jit(solution)/shard_map/sqhd,skd->shqk/dot_general | solution.py:135
  108.1 8.1 %fusion.3 = f32[2,4,512]{2,1,0:T(4,128)S(1)} fusion(f32[2,4,512,1024]{2,3,1,0:T(8,128)} %get-tuple-element.165, f32[2,4,512]{2,1,0:T(4,128)S(1)} %get-tuple-element.164), kind=kLoop, calls=%fused_computation.11 | loop fusion | flops 8384512 | bytes 16809984 | tf_op jit(solution)/shard_map/reduce_sum | solution.py:143
  116.2 9.4 %fusion.50 = bf16[2,256,4,512]{3,1,2,0:T(8,128)(2,1)S(1)} fusion(f32[2,4,512,1024]{2,3,1,0:T(8,128)} %get-tuple-element.165, f32[2,4,512]{2,1,0:T(4,128)S(1)} %fusion.3, f32[2,4,512]{2,1,0:T(4,128)S(1)} %get-tuple-element.164, bf16[2,512,256]{2,1,0:T(8,128)(2,1)} %convolution_convert_fusion.1, bf16[2,512,256]{2,1,0:T(8,128)(2,1)} %collective-permute-done), kind=kOutput, calls=%fused_computation.102 | convolution fusion | flops 2163212288 | bytes 19955712 | tf_op jit(solution)/shard_map/shqk,skd->sqhd/dot_general | solution.py:146
  136.3 9.0 %fusion.45 = f32[2,512,2048]{2,1,0:T(8,128)} fusion(bf16[2,512,640]{2,1,0:T(8,128)(2,1)} %multiply_convert_fusion.2, bf16[640,2048]{1,0:T(8,128)(2,1)} %all-gather.11.cloned.1.call-done), kind=kOutput, calls=%fused_computation.83 | convolution fusion | flops 2684354560 | bytes 12320768 | tf_op jit(solution)/shard_map/sbd,df->sbf/dot_general | solution.py:165
  145.3 46.1 %all-gather.13.cloned.1.call-done = bf16[640,2048]{1,0:T(8,128)(2,1)} async-done(((bf16[160,2048]{1,0:T(8,128)(2,1)}), bf16[640,2048]{1,0:T(8,128)(2,1)}) %all-gather.13.cloned.1.call-update) | async-done | bytes 2621456 | tf_op jit(solution)/shard_map/all_gather | solution.py:162
  191.3 10.6 %multiply_convert_fusion.1 = (bf16[2,512,2048]{2,1,0:T(8,128)(2,1)}, f32[2,512,2048]{2,1,0:T(8,128)}) fusion(f32[2,512,2048]{2,1,0:T(8,128)} %fusion.45, bf16[2,512,640]{2,1,0:T(8,128)(2,1)} %multiply_convert_fusion.2, bf16[640,2048]{1,0:T(8,128)(2,1)} %all-gather.13.cloned.1.call-done), kind=kOutput, calls=%fused_computation.25 | convolution fusion | flops 2705326080 | bytes 24903680 | tf_op jit(solution)/shard_map/sbd,df->sbf/dot_general | solution.py:166
  202.0 44.4 %all-gather.15.cloned.1.call-done = bf16[2048,640]{1,0:T(8,128)(2,1)} async-done(((bf16[512,640]{1,0:T(8,128)(2,1)}), bf16[2048,640]{1,0:T(8,128)(2,1)}) %all-gather.15.cloned.1.call-update) | async-done | bytes 2621456 | tf_op jit(solution)/shard_map/all_gather | solution.py:163
  246.3 6.2 multiply_reduce_fusion.7
  255.6 12.3 %fusion.11 = (bf16[2,512,2048]{2,1,0:T(8,128)(2,1)S(1)}, bf16[2,512,2048]{2,1,0:T(8,128)(2,1)S(1)}) fusion(f32[2,512,2048]{2,1,0:T(8,128)} %fusion.45, f32[2,512,2048]{2,1,0:T(8,128)} %get-tuple-element.169, bf16[2,512,640]{2,1,0:T(8,128)(2,1)S(1)} %get-tuple-element.151, bf16[2048,640]{1,0:T(8,128)(2,1)S(1)} %copy-done.61), kind=kOutput, calls=%fused_computation.21 | convolution fusion | flops 2734686208 | bytes 29097984 | tf_op jit(solution)/shard_map/sbd,fd->sbf/dot_general | solution.py:182
  281.4 8.2 %fusion.53 = f32[2,1024,256]{2,1,0:T(8,128)S(1)} fusion(bf16[2,64,4,8,256]{4,3,2,1,0:T(8,128)(2,1)S(1)} %bitcast.178, f32[2,4,512,1024]{2,3,1,0:T(8,128)} %get-tuple-element.165, f32[2,4,512]{2,1,0:T(4,128)S(1)} %bitcast.181), kind=kOutput, calls=%fused_computation.106 | convolution fusion | flops 2155872256 | bytes 20987904 | tf_op jit(solution)/shard_map/shqk,sqhd->skd/dot_general | solution.py:220
  291.0 11.4 %fusion = (f32[2,4,512]{2,1,0:T(4,128)S(1)}, f32[2,1024,512,4]{2,1,3,0:T(8,128)}) fusion(f32[2,4,512,1024]{2,3,1,0:T(8,128)} %get-tuple-element.165, f32[2,4,512]{2,1,0:T(4,128)S(1)} %bitcast.182, bf16[2,64,4,8,256]{4,3,2,1,0:T(8,128)(2,1)S(1)} %bitcast.179, bf16[2,512,256]{2,1,0:T(8,128)(2,1)} %convolution_convert_fusion.1, ...), kind=kOutput, calls=%fused_computation.4 | convolution fusion | flops 2162159616 | bytes 36732928 | tf_op jit(solution)/shard_map/sqhd,skd->shqk/dot_general | solution.py:207
  302.4 11.8 %fusion.2 = bf16[2,4,512,1024]{2,3,1,0:T(8,128)(2,1)S(1)} fusion(f32[2,1024,512,4]{2,1,3,0:T(8,128)} %get-tuple-element.174, f32[2,4,512,1024]{2,3,1,0:T(8,128)} %get-tuple-element.165, f32[2,4,512]{2,1,0:T(4,128)S(1)} %get-tuple-element.173, f32[2,4,512]{2,1,0:T(4,128)S(1)} %bitcast.183), kind=kLoop, calls=%fused_computation.6 | loop fusion | flops 16777216 | bytes 41975808 | tf_op jit(solution)/shard_map/convert_element_type | solution.py:211
  340.8 6.0 bitcast_multiply_fusion.1
  359.5 6.6 bitcast_convert_fusion
  367.4 6.7 bitcast_convert_fusion.2
  374.4 6.6 bitcast_convert_fusion.1
  382.8 12.0 %reduce-scatter.23.cloned.1.call-done = bf16[640,32]{0,1:T(8,128)(2,1)} async-done(((bf16[640,256]{0,1:T(8,128)(2,1)}), bf16[640,32]{0,1:T(8,128)(2,1)}) %reduce-scatter.23.cloned.1.call-update) | async-done | bytes 40976 | tf_op jit(solution)/shard_map/reduce_scatter | solution.py:259
  396.4 38.9 %reduce-scatter.27.cloned.1.call-done = bf16[1024,80]{0,1:T(8,128)(2,1)} async-done(((bf16[1024,640]{0,1:T(8,128)(2,1)}), bf16[1024,80]{0,1:T(8,128)(2,1)}) %reduce-scatter.27.cloned.1.call-update) | async-done | bytes 163856 | tf_op jit(solution)/shard_map/reduce_scatter | solution.py:265
  435.4 40.5 %reduce-scatter.43.cloned.1.call-done = bf16[128,640]{1,0:T(8,128)(2,1)} async-done(((bf16[1024,640]{1,0:T(8,128)(2,1)}), bf16[128,640]{1,0:T(8,128)(2,1)}) %reduce-scatter.43.cloned.1.call-update) | async-done | bytes 163856
  477.7 45.1 %reduce-scatter.39.cloned.1.call-done = bf16[2048,80]{0,1:T(8,128)(2,1)} async-done(((bf16[2048,640]{0,1:T(8,128)(2,1)}), bf16[2048,80]{0,1:T(8,128)(2,1)}) %reduce-scatter.39.cloned.1.call-update) | async-done | bytes 327696 | tf_op jit(solution)/shard_map/reduce_scatter | solution.py:274
  522.9 46.9 %reduce-scatter.31.cloned.1.call-done = bf16[640,256]{1,0:T(8,128)(2,1)} async-done(((bf16[640,2048]{1,0:T(8,128)(2,1)}), bf16[640,256]{1,0:T(8,128)(2,1)}) %reduce-scatter.31.cloned.1.call-update) | async-done | bytes 327696 | tf_op jit(solution)/shard_map/reduce_scatter | solution.py:268
  575.3 41.3 %reduce-scatter.35.cloned.1.call-done = bf16[640,256]{1,0:T(8,128)(2,1)} async-done(((bf16[640,2048]{1,0:T(8,128)(2,1)}), bf16[640,256]{1,0:T(8,128)(2,1)}) %reduce-scatter.35.cloned.1.call-update) | async-done | bytes 327696 | tf_op jit(solution)/shard_map/reduce_scatter | solution.py:271
  616.7 5.9 fusion.26
  622.6 39.9 %all-reduce.5 = (f32[640]{0:T(1024)}, f32[640]{0:T(1024)}, f32[640]{0:T(1024)}, f32[640]{0:T(1024)}, f32[256]{0:T(256)}, /*index=5*/f32[256]{0:T(256)}) all-reduce(f32[640]{0:T(1024)S(1)} %get-tuple-element.118, f32[640]{0:T(1024)S(1)} %get-tuple-element.114, ...), channel_id=1, replica_groups=mesh['seq'=8,'fsdp'=4] {'seq','fsdp'}, use_global_device_ids=true, to_apply=%region_35.36 | all-reduce | flops 3072 | bytes 24576 | tf_op jit(solution)/shard_map/psum | solution.py:301
  669.4 9.3 %reduce-scatter.29.cloned.1.call-done = bf16[256,80]{0,1:T(8,128)(2,1)} async-done(((bf16[1024,80]{0,1:T(8,128)(2,1)}), bf16[256,80]{0,1:T(8,128)(2,1)}) %reduce-scatter.29.cloned.1.call-update) | async-done | bytes 40976 | tf_op jit(solution)/shard_map/reduce_scatter | solution.py:288
  680.1 18.9 %reduce-scatter.21.cloned.1.call-done = bf16[160,128]{1,0:T(8,128)(2,1)} async-done(((bf16[640,128]{1,0:T(8,128)(2,1)}), bf16[160,128]{1,0:T(8,128)(2,1)}) %reduce-scatter.21.cloned.1.call-update) | async-done | bytes 40976 | tf_op jit(solution)/shard_map/reduce_scatter | solution.py:279
  700.4 18.8 %reduce-scatter.41.cloned.1.call-done = bf16[512,80]{0,1:T(8,128)(2,1)} async-done(((bf16[2048,80]{0,1:T(8,128)(2,1)}), bf16[512,80]{0,1:T(8,128)(2,1)}) %reduce-scatter.41.cloned.1.call-update) | async-done | bytes 81936 | tf_op jit(solution)/shard_map/reduce_scatter | solution.py:297
  720.8 18.9 %reduce-scatter.33.cloned.1.call-done = bf16[160,256]{1,0:T(8,128)(2,1)} async-done(((bf16[640,256]{1,0:T(8,128)(2,1)}), bf16[160,256]{1,0:T(8,128)(2,1)}) %reduce-scatter.33.cloned.1.call-update) | async-done | bytes 81936 | tf_op jit(solution)/shard_map/reduce_scatter | solution.py:291
  741.2 19.0 %reduce-scatter.37.cloned.1.call-done = bf16[160,256]{1,0:T(8,128)(2,1)} async-done(((bf16[640,256]{1,0:T(8,128)(2,1)}), bf16[160,256]{1,0:T(8,128)(2,1)}) %reduce-scatter.37.cloned.1.call-update) | async-done | bytes 81936 | tf_op jit(solution)/shard_map/reduce_scatter | solution.py:294
  (282 shorter events, 143.1 us)
Async XLA Ops:
  7.2 23.4 %copy-start.50 = (f32[640]{0:T(1024)S(1)}, f32[640]{0:T(1024)}, u32[]{:S(2)}) copy-start(f32[640]{0:T(1024)} %param.27) | copy-start | bytes 7684
  7.2 64.8 %all-gather.7.cloned.1.call-start = ((), (), s32[]{:S(2)}) async-start(), calls=%async_computation.14 | async-start | bytes 1638400 | tf_op jit(solution)/shard_map/all_gather | solution.py:99
  8.0 117.7 %all-gather.9.cloned.1.call-start = ((), (), s32[]{:S(2)}) async-start(), calls=%async_computation.15 | async-start | bytes 1638400 | tf_op jit(solution)/shard_map/all_gather | solution.py:102
  8.7 127.6 %all-gather.11.cloned.1.call-start = ((), (), s32[]{:S(2)}) async-start(), calls=%async_computation.16 | async-start | bytes 3276800 | tf_op jit(solution)/shard_map/all_gather | solution.py:161
  9.5 181.9 %all-gather.13.cloned.1.call-start = ((), (), s32[]{:S(2)}) async-start(), calls=%async_computation.17 | async-start | bytes 3276800 | tf_op jit(solution)/shard_map/all_gather | solution.py:162
  10.0 236.3 %all-gather.15.cloned.1.call-start = ((), (), s32[]{:S(2)}) async-start(), calls=%async_computation.18 | async-start | bytes 3276800 | tf_op jit(solution)/shard_map/all_gather | solution.py:163
  10.1 33.3 %copy-start.45 = (bf16[160,256]{1,0:T(8,128)(2,1)S(1)}, bf16[160,256]{1,0:T(8,128)(2,1)}, u32[]{:S(2)}) copy-start(bf16[160,256]{1,0:T(8,128)(2,1)} %param.21) | copy-start | bytes 245764
  32.1 29.1 %copy-start.51 = (f32[256]{0:T(256)S(1)}, f32[256]{0:T(256)}, u32[]{:S(2)}) copy-start(f32[256]{0:T(256)} %param.32) | copy-start | bytes 3076
  32.1 84.1 %collective-permute-start = (bf16[2,512,256]{2,1,0:T(8,128)(2,1)}, bf16[2,512,256]{2,1,0:T(8,128)(2,1)}, u32[]{:S(2)}, u32[]{:S(2)}) collective-permute-start(bf16[2,512,256]{2,1,0:T(8,128)(2,1)} %convolution_convert_fusion.1), channel_id=1, source_target_pairs={{0,4},{4,8},{8,12},{12,16},{16,20},{20,24},{24,28},{1,5},{5,9},{9,... | collective-permute-start | bytes 1572872 | tf_op jit(solution)/shard_map/ppermute | solution.py:29
  67.0 31.9 %collective-permute-start.1 = (bf16[2,512,256]{1,2,0:T(8,128)(2,1)}, bf16[2,512,256]{1,2,0:T(8,128)(2,1)S(1)}, u32[]{:S(2)}, u32[]{:S(2)}) collective-permute-start(bf16[2,512,256]{1,2,0:T(8,128)(2,1)} %get-tuple-element.159), channel_id=1, source_target_pairs={{0,4},{4,8},{8,12},{12,16},{16,20},{20,24},{24,28},{1,5},{5,9},{9,... | collective-permute-start | bytes 1572872 | tf_op jit(solution)/shard_map/ppermute | solution.py:29
  69.0 312.0 %reduce-scatter.25.cloned.1.call-start = ((), (), s32[]{:S(2)}) async-start(), calls=%async_computation.21 | async-start | bytes 368640 | tf_op jit(solution)/shard_map/reduce_scatter | solution.py:262
  289.7 30.6 %collective-permute-start.3 = (bf16[2,512,256]{2,1,0:T(8,128)(2,1)S(1)}, bf16[2,512,256]{2,1,0:T(8,128)(2,1)S(1)}, u32[]{:S(2)}, u32[]{:S(2)}) collective-permute-start(bf16[2,512,256]{2,1,0:T(8,128)(2,1)S(1)} %slice.66), channel_id=1, source_target_pairs={{4,0},{8,4},{12,8},{16,12},{20,16},{24,20},{28,24},{5,1},{9,5},{13... | collective-permute-start | bytes 1572872 | tf_op jit(solution)/shard_map/ppermute | solution.py:29
  319.0 4.7 collective-permute-start.2
  323.3 71.4 %reduce-scatter.23.cloned.1.call-start = ((), (), s32[]{:S(2)}) async-start(), calls=%async_computation.20 | async-start | bytes 368640 | tf_op jit(solution)/shard_map/reduce_scatter | solution.py:259
  336.0 99.3 %reduce-scatter.27.cloned.1.call-start = ((), (), s32[]{:S(2)}) async-start(), calls=%async_computation.22 | async-start | bytes 1474560 | tf_op jit(solution)/shard_map/reduce_scatter | solution.py:265
  340.8 135.1 %reduce-scatter.43.cloned.1.call-start = ((), (), s32[]{:S(2)}) async-start(), calls=%async_computation.30 | async-start | bytes 1474560
  359.4 163.4 %reduce-scatter.39.cloned.1.call-start = ((), (), s32[]{:S(2)}) async-start(), calls=%async_computation.28 | async-start | bytes 2949120 | tf_op jit(solution)/shard_map/reduce_scatter | solution.py:274
  366.1 203.7 %reduce-scatter.31.cloned.1.call-start = ((), (), s32[]{:S(2)}) async-start(), calls=%async_computation.24 | async-start | bytes 2949120 | tf_op jit(solution)/shard_map/reduce_scatter | solution.py:268
  374.1 242.6 %reduce-scatter.35.cloned.1.call-start = ((), (), s32[]{:S(2)}) async-start(), calls=%async_computation.26 | async-start | bytes 2949120 | tf_op jit(solution)/shard_map/reduce_scatter | solution.py:271
  381.0 188.9 %copy-start.31 = (bf16[640,256]{1,0:T(8,128)(2,1)S(1)}, bf16[640,256]{1,0:T(8,128)(2,1)}, u32[]{:S(2)}) copy-start(bf16[640,256]{1,0:T(8,128)(2,1)} %copy-done.30) | copy-start | bytes 983044
  381.0 285.4 %reduce-scatter.47.cloned.1.call-start = ((), (), s32[]{:S(2)}) async-start(), calls=%async_computation.32 | async-start | bytes 204800
  382.7 189.3 %copy-start.23 = (bf16[2,512,4,256]{1,3,2,0:T(8,128)(2,1)S(1)}, bf16[2,512,4,256]{1,3,2,0:T(8,128)(2,1)}, u32[]{:S(2)}) copy-start(bf16[2,512,4,256]{1,3,2,0:T(8,128)(2,1)} %copy-done.22) | copy-start | bytes 6291460
  382.7 285.2 %reduce-scatter.45.cloned.1.call-start = ((), (), s32[]{:S(2)}) async-start(), calls=%async_computation.31 | async-start | bytes 204800
  396.3 282.3 %reduce-scatter.29.cloned.1.call-start = ((), (), s32[]{:S(2)}) async-start(), calls=%async_computation.23 | async-start | bytes 204800 | tf_op jit(solution)/shard_map/reduce_scatter | solution.py:288
  435.3 263.6 %reduce-scatter.21.cloned.1.call-start = ((), (), s32[]{:S(2)}) async-start(), calls=%async_computation.19 | async-start | bytes 204800 | tf_op jit(solution)/shard_map/reduce_scatter | solution.py:279
  477.6 241.6 %reduce-scatter.41.cloned.1.call-start = ((), (), s32[]{:S(2)}) async-start(), calls=%async_computation.29 | async-start | bytes 409600 | tf_op jit(solution)/shard_map/reduce_scatter | solution.py:297
  522.8 216.8 %reduce-scatter.33.cloned.1.call-start = ((), (), s32[]{:S(2)}) async-start(), calls=%async_computation.25 | async-start | bytes 409600 | tf_op jit(solution)/shard_map/reduce_scatter | solution.py:291
  569.8 190.3 %reduce-scatter.37.cloned.1.call-start = ((), (), s32[]{:S(2)}) async-start(), calls=%async_computation.27 | async-start | bytes 409600 | tf_op jit(solution)/shard_map/reduce_scatter | solution.py:294
  572.0 44.7 %copy-start.25 = (bf16[640,256]{1,0:T(8,128)(2,1)S(1)}, bf16[640,256]{1,0:T(8,128)(2,1)}, u32[]{:S(2)}) copy-start(bf16[640,256]{1,0:T(8,128)(2,1)} %copy-done.24) | copy-start | bytes 983044
  572.0 44.7 %copy-start.37 = (bf16[2,512,256]{2,1,0:T(8,128)(2,1)S(1)}, bf16[2,512,256]{2,1,0:T(8,128)(2,1)}, u32[]{:S(2)}) copy-start(bf16[2,512,256]{2,1,0:T(8,128)(2,1)} %copy-done.36) | copy-start | bytes 1572868
  616.7 45.8 %copy-start.47 = (f32[2,512]{1,0:T(2,128)S(1)}, f32[2,512]{1,0:T(2,128)}, u32[]{:S(2)}) copy-start(f32[2,512]{1,0:T(2,128)} %copy-done.46) | copy-start | bytes 12292
  616.7 45.8 %copy-start.4 = (f32[2,512,640]{2,1,0:T(8,128)S(1)}, f32[2,512,640]{2,1,0:T(8,128)}, u32[]{:S(2)}) copy-start(f32[2,512,640]{2,1,0:T(8,128)} %copy-done.3) | copy-start | bytes 7864324
  (59 other events, 302.9 us)
Sparse Core Ops, SparseCore 0:
  9.6 37.3 all-gather.6
  48.6 31.6 all-gather.8
  81.8 54.3 all-gather.10
  137.7 53.5 all-gather.12
  192.7 53.5 all-gather.14
  323.4 34.4 reduce-scatter.24
  360.9 33.7 reduce-scatter.22
  398.0 37.2 reduce-scatter.26
  438.5 37.2 reduce-scatter.42
  479.0 43.6 reduce-scatter.38
  526.1 43.6 reduce-scatter.30
  573.0 43.6 reduce-scatter.34
  619.5 19.2 reduce-scatter.46
  641.6 17.5 reduce-scatter.44
  661.2 17.3 reduce-scatter.28
  681.4 17.4 reduce-scatter.20
  701.1 18.0 reduce-scatter.40
  721.3 18.2 reduce-scatter.32
  741.9 18.2 reduce-scatter.36
where the time goes:
time: 774 us; the launch traced here: 769 us
  waiting for transfers between devices  407 us (53%)
  matrix products  148 us (19%)
  blocking collectives  81.6 us (11%)
  other arithmetic  72.6 us (9%)
  local copies, waits for them, and re-layouts  34.5 us (4%)
  between operations  16.1 us (2%)
  starting transfers between devices  8.38 us (1%)
    reduce_scatter x1, waiting for transfers between devices, body(): lax.psum_scatter(part_gate.astype(jnp.bfloat16), 'seq', scatter_dimension...  46.9 us
    all_gather x1, waiting for transfers between devices, body(): lax.all_gather(w_up, 'fsdp', axis=0, tiled=True)  46.1 us
    reduce_scatter x1, waiting for transfers between devices, body(): lax.psum_scatter(part_down.astype(jnp.bfloat16), 'seq', scatter_dimension...  45.1 us
    all_gather x1, waiting for transfers between devices, body(): lax.all_gather(w_down, 'fsdp', axis=0, tiled=True)  44.4 us
    unnamed x22, waiting for transfers between devices  43.3 us
    reduce_scatter x1, waiting for transfers between devices, body(): lax.psum_scatter(part_up.astype(jnp.bfloat16), 'seq', scatter_dimension=1...  41.3 us
    psum x1, blocking collectives, body(): lax.psum((gp_attnpre, gp_attnpost, gp_ffnpre, gp_ffnpost, gp_query, gp_ke...  39.9 us
    reduce_scatter x1, waiting for transfers between devices, body(): lax.psum_scatter(part_out.astype(jnp.bfloat16), 'seq', scatter_dimension=...  38.9 us
  transfers between devices with their start and end apart: 23, of which 15 were waited for; matrix products, arithmetic and copies ran while one was open for 26% of the time, Pallas kernels for 0%

commit v1 on v0

v1 whole, which is shorter than its diff:
```python
import functools

import jax
import jax.numpy as jnp
from jax import lax
from jax.experimental import pallas as pl
from jax.experimental.pallas import tpu as pltpu
from jax.sharding import PartitionSpec as P

WINDOW = 512
TILE = 128
FF_TILE = 256
FFN_ROWS = 256

epsilon = 1e-06
NEG_FILL = -1e30
ROPE_BASE = 10000.0
GELU_C = 0.7978845608028654
GELU_K = 0.044715

f32 = jnp.float32
bf16 = jnp.bfloat16

NN = (((1,), (0,)), ((), ()))
NT = (((1,), (1,)), ((), ()))
TN = (((0,), (0,)), ((), ()))


def mm(left, right, dims=NN):
    return lax.dot_general(left, right, dims, preferred_element_type=f32)


def inv_rms(vector):
    return lax.rsqrt(jnp.mean(vector * vector, axis=-1, keepdims=True) + epsilon)


def norm_back(vector, inv, gain, grad):
    unit = vector * inv
    scaled = gain * grad
    back = inv * (scaled - unit * jnp.mean(unit * scaled, axis=-1, keepdims=True))
    return back, grad * unit


def rope(vector, cosine, sine):
    half = vector.shape[-1] // 2
    one, two = vector[:, :half], vector[:, half:]
    return jnp.concatenate([one * cosine - two * sine, two * cosine + one * sine], axis=1)


def rope_back(vector, cosine, sine):
    half = vector.shape[-1] // 2
    one, two = vector[:, :half], vector[:, half:]
    return jnp.concatenate([one * cosine + two * sine, two * cosine - one * sine], axis=1)


def params(limit_mib=56):
    return pltpu.CompilerParams(vmem_limit_bytes=limit_mib * 1024 * 1024)


def whole(shape):
    return pl.BlockSpec(shape, lambda *_: (0,) * len(shape))


def rows(count, width):
    return pl.BlockSpec((count, width), lambda i: (i, 0))


def shaped(shape, dtype):
    return jax.ShapeDtypeStruct(shape, dtype)


def qkv_kernel(
    tok_ref, far_ref, cos_ref, sin_ref, fcos_ref, fsin_ref, pack_ref, pre_ref, qn_ref, kn_ref,
    attn_ref, qraw_ref, qrot_ref, kraw_ref, key_ref, val_ref, wq_ref, wkv_ref, wot_ref,
):
    head_dim = kn_ref.shape[1]
    head_count = wq_ref.shape[1] // head_dim
    width = tok_ref.shape[1]
    block = tok_ref.shape[0]
    pieces, chunks, chunk_rows, _ = pack_ref.shape

    @pl.when(pl.program_id(0) == 0)
    def _():
        for s in range(pieces):
            wq_ref[:, s * 128 : (s + 1) * 128] = pack_ref[s, :, :, :128].reshape(width, 128)
        for s in range(0, pieces, 2):
            both = jnp.concatenate(
                [pack_ref[s + i, :, :, 256:320].reshape(width, 64) for i in range(2)], axis=1
            )
            wkv_ref[:, s * 64 : (s + 2) * 64] = both
        half = chunk_rows // 2
        for z in range(chunks):
            for i in range(2):
                part = pack_ref[:, z, i * half : (i + 1) * half, 128:256].reshape(width, 128)
                wot_ref[:, z * 256 + i * 128 : z * 256 + (i + 1) * 128] = part

    pre = pre_ref[...]
    kgain = kn_ref[...]
    token = tok_ref[...].astype(f32)
    low = (token * inv_rms(token) * pre).astype(bf16)
    attn_ref[...] = low
    query = mm(low, wq_ref[...])
    qraw_ref[...] = query
    cosine, sine = cos_ref[...], sin_ref[...]
    scaling = head_dim ** (-0.5)
    for h in range(head_count):
        part = query[:, h * head_dim : (h + 1) * head_dim]
        normed = part * inv_rms(part) * qn_ref[...]
        qrot_ref[:, h * head_dim : (h + 1) * head_dim] = (
            rope(normed, cosine, sine).astype(bf16) * jnp.asarray(scaling, bf16)
        )
    both = mm(low, wkv_ref[...])
    key = both[:, :head_dim]
    kraw_ref[...] = key
    key_ref[0, block:, :] = rope(key * inv_rms(key) * kgain, cosine, sine).astype(bf16)
    val_ref[0, block:, :] = both[:, head_dim:].astype(bf16)
    token = far_ref[...].astype(f32)
    low = (token * inv_rms(token) * pre).astype(bf16)
    both = mm(low, wkv_ref[...])
    key = both[:, :head_dim]
    key_ref[0, :block, :] = rope(key * inv_rms(key) * kgain, fcos_ref[...], fsin_ref[...]).astype(
        bf16
    )
    val_ref[0, :block, :] = both[:, head_dim:].astype(bf16)


def stacked(ref, tile, head_count, head_dim):
    return jnp.concatenate(
        [
            ref[tile * TILE : (tile + 1) * TILE, h * head_dim : (h + 1) * head_dim]
            for h in range(head_count)
        ],
        axis=0,
    )


def mask_of(pos_ref, tile, span):
    reach = jnp.minimum(pos_ref[tile * TILE : (tile + 1) * TILE, :], WINDOW - 1)
    row = lax.broadcasted_iota(jnp.int32, (TILE, span), 0)
    col = lax.broadcasted_iota(jnp.int32, (TILE, span), 1)
    distance = WINDOW + row - col
    return jnp.where((distance >= 0) & (distance <= reach), 0.0, NEG_FILL)


def attn_kernel(
    q_ref, key_ref, val_ref, pos_ref, tok_ref, wot_ref, post_ref, pre_ref,
    ctx_ref, lse_ref, branch_ref, res_ref, fin_ref,
):
    head_dim = key_ref.shape[2]
    head_count = q_ref.shape[1] // head_dim
    span = WINDOW + TILE
    lane = lax.broadcasted_iota(jnp.int32, (TILE, 128), 1)
    for tile in range(q_ref.shape[0] // TILE):
        query = stacked(q_ref, tile, head_count, head_dim)
        key = key_ref[0, tile * TILE : tile * TILE + span, :]
        value = val_ref[0, tile * TILE : tile * TILE + span, :]
        score = mm(query, key, NT).reshape(head_count, TILE, span) + mask_of(pos_ref, tile, span)
        largest = jnp.max(score, axis=-1, keepdims=True)
        expo = jnp.exp(score - largest)
        total = jnp.sum(expo, axis=-1, keepdims=True)
        low = expo.astype(bf16).reshape(head_count * TILE, span)
        context = mm(low, value).reshape(head_count, TILE, head_dim) / total
        log_total = largest + jnp.log(total)
        kept = jnp.zeros((TILE, 128), f32)
        for h in range(head_count):
            ctx_ref[tile * TILE : (tile + 1) * TILE, h * head_dim : (h + 1) * head_dim] = context[
                h
            ].astype(bf16)
            kept = jnp.where(lane == h, log_total[h], kept)
        lse_ref[tile * TILE : (tile + 1) * TILE, :] = kept
    branch = mm(ctx_ref[...], wot_ref[...], NT)
    branch_ref[...] = branch
    residual = tok_ref[...].astype(f32) + branch * inv_rms(branch) * post_ref[...]
    res_ref[...] = residual
    fin_ref[...] = (residual * inv_rms(residual) * pre_ref[...]).astype(bf16)


def ffn_kernel(
    res_ref, fin_ref, cot_ref, branch_ref, wf_ref, wot_ref, postf_ref, pref_ref, posta_ref,
    out_ref, hid_ref, gg_ref, gu_ref, gffn_ref, gres_ref, gattn_ref, gctx_ref, gain_ref,
    slope_ref, act_ref,
):
    pieces, chunks, _, _ = wf_ref.shape
    width = res_ref.shape[1]
    quarter = width // chunks
    strip = width // pieces

    def gate_block(j):
        return wf_ref[j, :, :quarter, :].reshape(width, FF_TILE)

    def up_block(j):
        return wf_ref[j, :, quarter : 2 * quarter, :].reshape(width, FF_TILE)

    def down_block(j):
        start = 2 * quarter + (j % 2) * strip
        return wf_ref[:, j // 2, start : start + strip, :].reshape(width, FF_TILE)

    @pl.when(pl.program_id(0) == 0)
    def _():
        gain_ref[...] = jnp.zeros_like(gain_ref)

    ffn_in = fin_ref[...]
    branch = jnp.zeros(res_ref.shape, f32)
    for j in range(pieces):
        cols = slice(j * FF_TILE, (j + 1) * FF_TILE)
        gate = mm(ffn_in, gate_block(j))
        up = mm(ffn_in, up_block(j))
        square = gate * gate
        bent = jnp.tanh(GELU_C * gate * (1.0 + GELU_K * square))
        half = 0.5 * (1.0 + bent)
        act = gate * half
        slope = half + 0.5 * gate * (1.0 - bent * bent) * (
            GELU_C * (1.0 + 3.0 * GELU_K * square)
        )
        act_ref[:, cols] = act
        slope_ref[:, cols] = slope * up
        hidden = (act * up).astype(bf16)
        hid_ref[:, cols] = hidden
        branch += mm(hidden, down_block(j), NT)
    residual = res_ref[...]
    cot = cot_ref[...].astype(f32)
    inv = inv_rms(branch)
    out_ref[...] = (residual + branch * inv * postf_ref[...]).astype(bf16)
    g_ffn, gain_post = norm_back(branch, inv, postf_ref[...], cot)
    g_low = g_ffn.astype(bf16)
    gffn_ref[...] = g_low
    g_in = jnp.zeros(res_ref.shape, f32)
    for j in range(pieces):
        cols = slice(j * FF_TILE, (j + 1) * FF_TILE)
        g_hidden = mm(g_low, down_block(j))
        g_gate = (g_hidden * slope_ref[:, cols]).astype(bf16)
        g_up = (g_hidden * act_ref[:, cols]).astype(bf16)
        gg_ref[:, cols] = g_gate
        gu_ref[:, cols] = g_up
        g_in += mm(g_gate, gate_block(j), NT) + mm(g_up, up_block(j), NT)
    back, gain_pre = norm_back(residual, inv_rms(residual), pref_ref[...], g_in)
    g_res = cot + back
    gres_ref[...] = g_res
    attn_branch = branch_ref[...]
    g_attn, gain_attn = norm_back(attn_branch, inv_rms(attn_branch), posta_ref[...], g_res)
    g_attn = g_attn.astype(bf16)
    gattn_ref[...] = g_attn
    gctx_ref[...] = mm(g_attn, wot_ref[...]).astype(bf16)
    gain_ref[0:1, :] += jnp.sum(gain_post, axis=0, keepdims=True)
    gain_ref[1:2, :] += jnp.sum(gain_pre, axis=0, keepdims=True)
    gain_ref[2:3, :] += jnp.sum(gain_attn, axis=0, keepdims=True)


def down_kernel(gffn_ref, hid_ref, out_ref, left_ref):
    @pl.when(pl.program_id(0) == 0)
    def _():
        left_ref[...] = gffn_ref[...].T

    part = mm(left_ref[...], hid_ref[...]).astype(bf16)
    out_ref[...] = part.reshape(out_ref.shape)


def gate_kernel(fin_ref, gg_ref, gu_ref, out_ref, left_ref):
    @pl.when(pl.program_id(0) == 0)
    def _():
        left_ref[...] = fin_ref[...].T

    chunks, double, tile = out_ref.shape[1:]
    quarter = double // 2
    part = mm(left_ref[...], gg_ref[...]).astype(bf16)
    out_ref[0, :, :quarter, :] = part.reshape(chunks, quarter, tile)
    part = mm(left_ref[...], gu_ref[...]).astype(bf16)
    out_ref[0, :, quarter:, :] = part.reshape(chunks, quarter, tile)


def attn_back_kernel(
    q_ref, gctx_ref, key_ref, val_ref, pos_ref, lse_ref, qraw_ref, cos_ref, sin_ref, qn_ref,
    gq_ref, far_ref, near_ref, gain_ref, gkey_ref, gval_ref,
):
    head_dim = key_ref.shape[2]
    head_count = q_ref.shape[1] // head_dim
    block = q_ref.shape[0]
    span = WINDOW + TILE
    scaling = head_dim ** (-0.5)

    @pl.when(pl.program_id(0) == 0)
    def _():
        gain_ref[...] = jnp.zeros_like(gain_ref)

    gkey_ref[...] = jnp.zeros_like(gkey_ref)
    gval_ref[...] = jnp.zeros_like(gval_ref)
    gain = jnp.zeros((1, head_dim), f32)
    for tile in range(block // TILE):
        own = slice(tile * TILE, (tile + 1) * TILE)
        reach = slice(tile * TILE, tile * TILE + span)
        query = stacked(q_ref, tile, head_count, head_dim)
        g_ctx = stacked(gctx_ref, tile, head_count, head_dim)
        key = key_ref[0, reach, :]
        value = val_ref[0, reach, :]
        log_total = jnp.stack([lse_ref[own, h : h + 1] for h in range(head_count)])
        score = mm(query, key, NT).reshape(head_count, TILE, span) + mask_of(pos_ref, tile, span)
        probs = jnp.exp(score - log_total)
        g_probs = mm(g_ctx, value, NT).reshape(head_count, TILE, span)
        spread = jnp.sum(g_probs * probs, axis=-1, keepdims=True)
        g_score = (probs * (g_probs - spread)).astype(bf16).reshape(head_count * TILE, span)
        low = probs.astype(bf16).reshape(head_count * TILE, span)
        gkey_ref[reach, :] += mm(g_score, query, TN)
        gval_ref[reach, :] += mm(low, g_ctx, TN)
        g_rot = mm(g_score, key) * scaling
        cosine, sine = cos_ref[own, :], sin_ref[own, :]
        for h in range(head_count):
            cols = slice(h * head_dim, (h + 1) * head_dim)
            raw = qraw_ref[own, cols]
            back, share = norm_back(
                raw,
                inv_rms(raw),
                qn_ref[...],
                rope_back(g_rot[h * TILE : (h + 1) * TILE], cosine, sine),
            )
            gq_ref[own, cols] = back.astype(bf16)
            gain += jnp.sum(share, axis=0, keepdims=True)
    gain_ref[0:1, :] += gain
    far_ref[0, :, :head_dim] = gkey_ref[:block, :].astype(bf16)
    far_ref[0, :, head_dim:] = gval_ref[:block, :].astype(bf16)
    near_ref[0, :, :head_dim] = gkey_ref[block:, :]
    near_ref[0, :, head_dim:] = gval_ref[block:, :]


def input_kernel(
    near_ref, recv_ref, kraw_ref, cos_ref, sin_ref, gq_ref, wq_ref, wkv_ref, tok_ref, gres_ref,
    kn_ref, pre_ref,
    dtok_ref, gkv_ref, kgain_ref, gain_ref,
):
    head_dim = kn_ref.shape[1]

    @pl.when(pl.program_id(0) == 0)
    def _():
        gain_ref[...] = jnp.zeros_like(gain_ref)
        kgain_ref[...] = jnp.zeros_like(kgain_ref)

    both = near_ref[0] + recv_ref[0].astype(f32)
    raw = kraw_ref[...]
    g_key, share = norm_back(
        raw, inv_rms(raw), kn_ref[...], rope_back(both[:, :head_dim], cos_ref[...], sin_ref[...])
    )
    kgain_ref[0:1, :] += jnp.sum(share, axis=0, keepdims=True)
    gkv_ref[:, :head_dim] = g_key.astype(bf16)
    gkv_ref[:, head_dim:] = both[:, head_dim:].astype(bf16)
    g_in = mm(gq_ref[...], wq_ref[...], NT) + mm(gkv_ref[...], wkv_ref[...], NT)
    token = tok_ref[...].astype(f32)
    back, share = norm_back(token, inv_rms(token), pre_ref[...], g_in)
    dtok_ref[...] = (gres_ref[...] + back).astype(bf16)
    gain_ref[0:1, :] += jnp.sum(share, axis=0, keepdims=True)


def query_kernel(attn_ref, gq_ref, out_ref, left_ref):
    @pl.when(pl.program_id(0) == 0)
    def _():
        left_ref[...] = attn_ref[...].T

    part = mm(left_ref[...], gq_ref[...]).astype(bf16)
    for i in range(out_ref.shape[0]):
        out_ref[i] = part[:, i * 128 : (i + 1) * 128].reshape(out_ref.shape[1:])


def kv_kernel(attn_ref, gkv_ref, out_ref):
    out_ref[...] = mm(attn_ref[...].T, gkv_ref[...]).astype(bf16)


def carried_in(value, axis, join, neutral):
    count, mine = (lax.axis_size(axis), lax.axis_index(axis))
    pieces = lax.all_gather(value, axis)
    subtotal = jnp.full_like(value, 0) + jnp.asarray(neutral, value.dtype)

    def step(position, subtotal):
        longer = join(subtotal, pieces[position])
        return jnp.where(position < mine, longer, subtotal)

    return lax.fori_loop(0, count - 1, step, subtotal)


def passed_along(shard, axis, by):
    length = lax.axis_size(axis)
    pairs = [(i, i + by) for i in range(length) if 0 <= i + by < length]
    return lax.ppermute(shard, axis, pairs)


def tables(positions, head_dim):
    half_width = head_dim // 2
    frequency = ROPE_BASE ** (-(jnp.arange(half_width, dtype=f32) * 2.0) / head_dim)
    angles = positions.astype(f32)[..., None] * frequency
    return (jnp.cos(angles), jnp.sin(angles))


def column_piece(array, axis_name, parts):
    wide = array.shape[1] // parts
    return lax.dynamic_slice_in_dim(array, lax.axis_index(axis_name) * wide, wide, 1)


def gathered(piece):
    return lax.all_gather(piece, ("seq", "fsdp"), axis=0, tiled=False)


def scattered(parts):
    over_seq = lax.psum_scatter(parts, "seq", scatter_dimension=0, tiled=True)
    return lax.psum_scatter(over_seq[0], "fsdp", scatter_dimension=0, tiled=True)[0]


def scattered_plain(part):
    columns = lax.psum_scatter(part, "seq", scatter_dimension=1, tiled=True)
    return lax.psum_scatter(columns, "fsdp", scatter_dimension=0, tiled=True).astype(f32)


def gather_weights(w_query, w_key, w_value, w_out, w_gate, w_up, w_down, seqs, chunks):
    pieces = w_gate.shape[1] // FF_TILE
    width = w_out.shape[1]
    if pieces == seqs and w_down.shape[0] == 2 * FF_TILE:
        both = jnp.concatenate([w_key, w_value], axis=1)
        out = column_piece(w_out, "seq", seqs).T
        out = jnp.concatenate([out[:, :128], out[:, 128:]], axis=0)
        attn = jnp.concatenate(
            [column_piece(w_query, "seq", seqs), out, column_piece(both, "seq", seqs)], axis=1
        )
        down = column_piece(w_down, "seq", seqs).T
        ffn = jnp.concatenate(
            [
                column_piece(w_gate, "seq", seqs),
                column_piece(w_up, "seq", seqs),
                down[:, :FF_TILE],
                down[:, FF_TILE:],
            ],
            axis=0,
        )
        shape = (seqs, chunks)
        attn = gathered(attn)
        attn, ffn = lax.optimization_barrier((attn, ffn))
        ffn = gathered(ffn)
        return attn.reshape(shape + attn.shape[1:]), ffn.reshape(shape + ffn.shape[1:])
    w_query, w_key, w_value, w_out, w_gate, w_up, w_down = [
        lax.all_gather(w, "fsdp", axis=0, tiled=True)
        for w in (w_query, w_key, w_value, w_out, w_gate, w_up, w_down)
    ]
    chunks = w_down.shape[0] // (2 * FF_TILE)
    quarter, strip = width // chunks, width // pieces

    def columns(weight):
        return weight.reshape(chunks, quarter, pieces, -1).transpose(2, 0, 1, 3)

    def turned(weight):
        shape = (pieces, strip, chunks, 2, weight.shape[0] // (2 * chunks))
        turned_part = weight.T.reshape(shape).transpose(0, 2, 3, 1, 4)
        return turned_part.reshape(pieces, chunks, 2 * strip, -1)

    both = jnp.concatenate([w_key, w_value], axis=1)
    attn = jnp.concatenate([columns(w_query), turned(w_out), columns(both)], axis=3)
    ffn = jnp.concatenate([columns(w_gate), columns(w_up), turned(w_down)], axis=2)
    return attn, ffn


def scatter_gradients(part_gate, part_down, part_out, part_query, part_kv, seqs, chunks):
    pieces, quarters, _, _ = part_gate.shape
    width = part_kv.shape[0]
    quarter, strip = width // quarters, width // pieces
    head_dim = part_kv.shape[1] // 2
    if pieces == seqs and quarters == chunks:
        both = part_kv.reshape(quarters, quarter, 2, pieces, head_dim // pieces)
        both = both.transpose(3, 0, 1, 2, 4).reshape(pieces, quarters, quarter, -1)
        part_attn = jnp.concatenate([part_query, both], axis=3)
        down = scattered(part_down)
        out = scattered(part_out)
        gate = scattered(part_gate)
        attn = scattered(part_attn)
        down = jnp.concatenate([down[:strip], down[strip:]], axis=1)
        return (
            attn[:, :128].astype(f32),
            attn[:, 128 : 128 + head_dim // pieces].astype(f32),
            attn[:, 128 + head_dim // pieces :].astype(f32),
            out.astype(f32).T,
            gate[:quarter].astype(f32),
            gate[quarter:].astype(f32),
            down.astype(f32).T,
        )

    def columns(parts):
        return parts.transpose(1, 2, 0, 3).reshape(width, -1)

    down = part_down.reshape(pieces, quarters, 2, strip, FF_TILE).transpose(1, 2, 4, 0, 3)
    out = part_out.transpose(1, 3, 0, 2)
    return tuple(
        scattered_plain(part)
        for part in (
            columns(part_query),
            part_kv[:, :head_dim],
            part_kv[:, head_dim:],
            out.reshape(-1, width),
            columns(part_gate[:, :, :quarter]),
            columns(part_gate[:, :, quarter:]),
            down.reshape(-1, width),
        )
    )


def body(
    tokens, doc_starts, w_query, w_key, w_value, w_out, w_gate, w_up, w_down,
    pre_attn, post_attn, pre_ffn, post_ffn, query_norm, key_norm, cotangent,
):
    seq_dev, block, width = tokens.shape
    head_dim = w_key.shape[1]
    inner = w_query.shape[1]
    hidden_dim = w_gate.shape[1]
    count = seq_dev * block
    seqs, chunks = lax.axis_size("seq"), lax.axis_size("fsdp")
    offset = lax.axis_index("seq") * block
    indices = offset + jnp.arange(block, dtype=jnp.int32)
    marked = jnp.where(doc_starts == 1, indices[None, :], -1)
    before = carried_in(
        jnp.max(marked, axis=1), "seq", jnp.maximum, jnp.full((seq_dev,), -1, jnp.int32)
    )
    latest = jnp.maximum(lax.cummax(marked, axis=1), before[:, None])
    positions = indices[None, :] - latest
    far_tokens = passed_along(tokens, "seq", 1).reshape(count, width)
    far_positions = passed_along(positions, "seq", 1)
    cosine, sine = tables(positions.reshape(count), head_dim)
    far_cosine, far_sine = tables(far_positions.reshape(count), head_dim)
    pos_column = positions.reshape(count, 1)

    pack, ffn_pack = gather_weights(
        w_query, w_key, w_value, w_out, w_gate, w_up, w_down, seqs, chunks
    )
    pieces, quarters = ffn_pack.shape[:2]
    quarter, strip = width // quarters, width // pieces
    gains = [g.reshape(1, -1) for g in (pre_attn, post_attn, pre_ffn, post_ffn)]
    pre_attn, post_attn, pre_ffn, post_ffn = gains
    query_norm, key_norm = query_norm.reshape(1, -1), key_norm.reshape(1, -1)
    tokens_2d = tokens.reshape(count, width)
    cot_2d = cotangent.reshape(count, width)

    tok_spec = rows(block, width)
    half_spec = rows(block, head_dim // 2)
    key_spec = pl.BlockSpec((1, 2 * block, head_dim), lambda i: (i, 0, 0))
    gain_w, gain_h = whole((1, width)), whole((1, head_dim))
    wq_spec, wkv_spec, wot_spec = (
        whole((width, inner)),
        whole((width, 2 * head_dim)),
        whole((width, inner)),
    )
    attn_low, query_raw, query_rot, key_raw, keys, values, full_q, full_kv, full_ot = (
        pl.pallas_call(
            qkv_kernel,
            grid=(seq_dev,),
            in_specs=[tok_spec, tok_spec, half_spec, half_spec, half_spec, half_spec]
            + [whole(pack.shape), gain_w, gain_h, gain_h],
            out_specs=[
                tok_spec,
                rows(block, inner),
                rows(block, inner),
                rows(block, head_dim),
                key_spec,
                key_spec,
                wq_spec,
                wkv_spec,
                wot_spec,
            ],
            out_shape=[
                shaped((count, width), bf16),
                shaped((count, inner), f32),
                shaped((count, inner), bf16),
                shaped((count, head_dim), f32),
                shaped((seq_dev, 2 * block, head_dim), bf16),
                shaped((seq_dev, 2 * block, head_dim), bf16),
                shaped((width, inner), bf16),
                shaped((width, 2 * head_dim), bf16),
                shaped((width, inner), bf16),
            ],
            compiler_params=params(),
            name="project_rotate",
        )(
            tokens_2d, far_tokens, cosine, sine, far_cosine, far_sine, pack,
            pre_attn, query_norm, key_norm,
        )
    )
    context, log_total, attn_branch, residual, ffn_in = pl.pallas_call(
        attn_kernel,
        grid=(seq_dev,),
        in_specs=[rows(block, inner), key_spec, key_spec, rows(block, 1), tok_spec]
        + [wot_spec, gain_w, gain_w],
        out_specs=[rows(block, inner), rows(block, 128), tok_spec, tok_spec, tok_spec],
        out_shape=[
            shaped((count, inner), bf16),
            shaped((count, 128), f32),
            shaped((count, width), f32),
            shaped((count, width), f32),
            shaped((count, width), bf16),
        ],
        compiler_params=params(),
        name="window_attention",
    )(query_rot, keys, values, pos_column, tokens_2d, full_ot, post_attn, pre_ffn)

    small = rows(FFN_ROWS, width)
    wide = rows(FFN_ROWS, hidden_dim)
    layer_out, hidden, g_gate, g_up, g_ffn, g_res, g_attn, g_ctx, ffn_gains = pl.pallas_call(
        ffn_kernel,
        grid=(count // FFN_ROWS,),
        in_specs=[small, small, small, small, whole(ffn_pack.shape), wot_spec]
        + [gain_w, gain_w, gain_w],
        out_specs=[small, wide, wide, wide, small, small, small, rows(FFN_ROWS, inner)]
        + [whole((8, width))],
        out_shape=[
            shaped((count, width), bf16),
            shaped((count, hidden_dim), bf16),
            shaped((count, hidden_dim), bf16),
            shaped((count, hidden_dim), bf16),
            shaped((count, width), bf16),
            shaped((count, width), f32),
            shaped((count, width), bf16),
            shaped((count, inner), bf16),
            shaped((8, width), f32),
        ],
        scratch_shapes=[
            pltpu.VMEM((FFN_ROWS, hidden_dim), f32),
            pltpu.VMEM((FFN_ROWS, hidden_dim), f32),
        ],
        compiler_params=params(),
        name="feed_forward",
    )(residual, ffn_in, cot_2d, attn_branch, ffn_pack, full_ot, post_ffn, pre_ffn, post_attn)

    full_rows = whole((count, width))
    ff_cols = pl.BlockSpec((count, FF_TILE), lambda j: (0, j))
    left_scratch = [pltpu.VMEM((width, count), bf16)]
    part_down = pl.pallas_call(
        down_kernel,
        grid=(pieces,),
        in_specs=[full_rows, ff_cols],
        out_specs=pl.BlockSpec((pieces, 1, strip, FF_TILE), lambda j: (0, j // 2, j % 2, 0)),
        out_shape=shaped((pieces, quarters, 2 * strip, FF_TILE), bf16),
        scratch_shapes=left_scratch,
        compiler_params=params(),
        name="down_gradient",
    )(g_ffn, hidden)
    part_gate = pl.pallas_call(
        gate_kernel,
        grid=(pieces,),
        in_specs=[full_rows, ff_cols, ff_cols],
        out_specs=pl.BlockSpec((1, quarters, 2 * quarter, FF_TILE), lambda j: (j, 0, 0, 0)),
        out_shape=shaped((pieces, quarters, 2 * quarter, FF_TILE), bf16),
        scratch_shapes=left_scratch,
        compiler_params=params(),
        name="gate_up_gradient",
    )(ffn_in, g_gate, g_up)
    part_out = pl.pallas_call(
        down_kernel,
        grid=(quarters,),
        in_specs=[full_rows, ff_cols],
        out_specs=pl.BlockSpec((pieces, 1, strip, FF_TILE), lambda j: (0, j, 0, 0)),
        out_shape=shaped((pieces, quarters, strip, FF_TILE), bf16),
        scratch_shapes=left_scratch,
        compiler_params=params(),
        name="out_gradient",
    )(g_attn, context)

    kv_spec = pl.BlockSpec((1, block, 2 * head_dim), lambda i: (i, 0, 0))
    g_query, g_far, g_near, query_gain = pl.pallas_call(
        attn_back_kernel,
        grid=(seq_dev,),
        in_specs=[rows(block, inner), rows(block, inner), key_spec, key_spec, rows(block, 1)]
        + [rows(block, 128), rows(block, inner), half_spec, half_spec, gain_h],
        out_specs=[rows(block, inner), kv_spec, kv_spec, whole((8, head_dim))],
        out_shape=[
            shaped((count, inner), bf16),
            shaped((seq_dev, block, 2 * head_dim), bf16),
            shaped((seq_dev, block, 2 * head_dim), f32),
            shaped((8, head_dim), f32),
        ],
        scratch_shapes=[
            pltpu.VMEM((2 * block, head_dim), f32),
            pltpu.VMEM((2 * block, head_dim), f32),
        ],
        compiler_params=params(),
        name="attention_gradient",
    )(
        query_rot, g_ctx, keys, values, pos_column, log_total, query_raw, cosine, sine, query_norm
    )
    g_recv = passed_along(g_far, "seq", -1)
    part_query = pl.pallas_call(
        query_kernel,
        grid=(inner // 256,),
        in_specs=[full_rows, ff_cols],
        out_specs=pl.BlockSpec((2, quarters, quarter, 128), lambda j: (j, 0, 0, 0)),
        out_shape=shaped((inner // 128, quarters, quarter, 128), bf16),
        scratch_shapes=left_scratch,
        compiler_params=params(),
        name="query_gradient",
    )(attn_low, g_query)
    dtokens, g_kv, key_gain, attn_gain = pl.pallas_call(
        input_kernel,
        grid=(seq_dev,),
        in_specs=[kv_spec, kv_spec, rows(block, head_dim), half_spec, half_spec]
        + [rows(block, inner), wq_spec, wkv_spec, tok_spec, tok_spec, gain_h, gain_w],
        out_specs=[tok_spec, rows(block, 2 * head_dim), whole((8, head_dim)), whole((8, width))],
        out_shape=[
            shaped((count, width), bf16),
            shaped((count, 2 * head_dim), bf16),
            shaped((8, head_dim), f32),
            shaped((8, width), f32),
        ],
        compiler_params=params(),
        name="input_gradient",
    )(
        g_near, g_recv, key_raw, cosine, sine, g_query, full_q, full_kv, tokens_2d, g_res,
        key_norm, pre_attn,
    )
    part_kv = pl.pallas_call(
        kv_kernel,
        out_shape=shaped((width, 2 * head_dim), bf16),
        compiler_params=params(),
        name="key_value_gradient",
    )(attn_low, g_kv)

    weights = scatter_gradients(
        part_gate, part_down, part_out, part_query, part_kv, seqs, chunks
    )
    sums = lax.psum(
        jnp.concatenate(
            [attn_gain[0], ffn_gains[2], ffn_gains[1], ffn_gains[0], query_gain[0], key_gain[0]]
        ),
        ("seq", "fsdp"),
    )
    cuts = [0, width, 2 * width, 3 * width, 4 * width, 4 * width + head_dim]
    cuts.append(cuts[-1] + head_dim)
    gain_sums = tuple(sums[a:b] for a, b in zip(cuts[:-1], cuts[1:]))
    shape = (seq_dev, block, width)
    return (layer_out.reshape(shape), dtokens.reshape(shape)) + weights + gain_sums


def solution(mesh):
    sharded = P("fsdp", "seq", None)
    weight = P("fsdp", None)
    in_specs = (sharded, P("fsdp", "seq")) + (weight,) * 7 + (P(),) * 6 + (sharded,)
    out_specs = (sharded, sharded) + (P("fsdp", "seq"),) * 7 + (P(),) * 6
    return jax.shard_map(body, mesh=mesh, in_specs=in_specs, out_specs=out_specs, check_vma=False)
```

time: 774 us -> 504 us (0.65)
  matrix products: 148 us -> 0 us
  waiting for transfers between devices: 407 us -> 268 us
  Pallas kernels: 0 us -> 126 us
  other arithmetic: 72.6 us -> 18.1 us
  blocking collectives: 81.6 us -> 47.1 us
  local copies, waits for them, and re-layouts: 34.5 us -> 19.7 us
    dot_general x27 -> x0, matrix products: 148 us -> none  [the longest x1 12.3 us: body(): jnp.einsum('sbd,fd->sbf', g_ffnlow, full_down, preferred_element_type=jnp...]
    pallas_call x0 -> x10, Pallas kernels: none -> 126 us  [the longest x1 41.4 us: body(): pl.pallas_call(ffn_kernel, grid=(count // FFN_ROWS,), in_specs=[small, sm...]
    reduce_scatter x11 -> x8, waiting for transfers between devices: 269 us -> 177 us  [the longest x4 99.9 us: scattered(): over_seq = lax.psum_scatter(parts, 'seq', scatter_dimension=0, tiled=True)]
    unnamed x22 -> x10, waiting for transfers between devices: 43.3 us -> 0.82 us
    all_gather x2 -> x0, blocking collectives: 33.7 us -> none  [the longest x1 17.9 us: body(): lax.all_gather(w_value, 'fsdp', axis=0, tiled=True)]
    convert_element_type x17 -> x4, other arithmetic: 36.9 us -> 4.03 us  [the longest x1 1.67 us: scatter_gradients(): gate[quarter:].astype(f32)]
    reduce_sum x8 -> x0, other arithmetic: 22.8 us -> none  [the longest x4 10.2 us: norm_rows(): vector * lax.rsqrt(jnp.mean(vector * vector, axis=-1, keepdims=True) + ep...]
    unnamed x145 -> x39, local copies, waits for them, and re-layouts: 22.2 us -> 3.63 us
  transfers between devices with their start and end apart: 23 -> 13, of which waited for: 15 -> 9; matrix products, arithmetic and copies ran while one was open for 26% -> 6% of each run, Pallas kernels for 0% -> 16%
where the time goes in v1:
time: 504 us; the launch traced here: 503 us
  waiting for transfers between devices  268 us (53%)
  Pallas kernels  126 us (25%)
  blocking collectives  47.1 us (9%)
  local copies, waits for them, and re-layouts  19.7 us (4%)
  other arithmetic  18.1 us (4%)
  between operations  15.2 us (3%)
  starting transfers between devices  7.9 us (2%)
    reduce_scatter x4, waiting for transfers between devices, scattered(): over_seq = lax.psum_scatter(parts, 'seq', scatter_dimension=0, tiled=True)  99.9 us
    all_gather x2, waiting for transfers between devices, gathered(): return lax.all_gather(piece, ('seq', 'fsdp'), axis=0, tiled=False)  90 us
    reduce_scatter x4, waiting for transfers between devices, scattered(): lax.psum_scatter(over_seq[0], 'fsdp', scatter_dimension=0, tiled=True)[0]  77.4 us
    pallas_call x1, Pallas kernels, body(): pl.pallas_call(ffn_kernel, grid=(count // FFN_ROWS,), in_specs=[small, sm...  41.4 us
    psum x1, blocking collectives, body(): lax.psum(jnp.concatenate([attn_gain[0], ffn_gains[2], ffn_gains[1], ffn_g...  39.7 us
    pallas_call x1, Pallas kernels, body(): pl.pallas_call(attn_back_kernel, grid=(seq_dev,), in_specs=[rows(block, i...  16.4 us
    pallas_call x1, Pallas kernels, body(): pl.pallas_call(attn_kernel, grid=(seq_dev,), in_specs=[rows(block, inner)...  12.7 us
    pallas_call x1, Pallas kernels, body(): pl.pallas_call(gate_kernel, grid=(pieces,), in_specs=[full_rows, ff_cols,...  12.1 us
  transfers between devices with their start and end apart: 13, of which 9 were waited for; matrix products, arithmetic and copies ran while one was open for 6% of the time, Pallas kernels for 16%

profile of v1, /device:TPU:0, one launch (start us, length us, event | category | flops | bytes accessed | tf_op | source)
XLA Modules:
  0.0 502.7 jit_solution(187200658500091052)
XLA Ops:
  13.0 62.4 %all-gather.6.cloned.1.call-done = bf16[5120,320]{1,0:T(8,128)(2,1)} async-done(((bf16[160,320]{1,0:T(8,128)(2,1)}), bf16[5120,320]{1,0:T(8,128)(2,1)}) %all-gather.6.cloned.1.call-update) | async-done | bytes 3276816 | tf_op jit(solution)/shard_map/all_gather | solution.py:396
  77.2 7.3 %all-reduce = s32[16]{0:T(128)S(1)} all-reduce(s32[16]{0:T(128)S(1)} %dynamic-update-slice), channel_id=2, replica_groups=mesh['seq'=8,'fsdp'=4] {'seq'}, use_global_device_ids=true, to_apply=%add | all-reduce | flops 16 | bytes 128
  86.0 1.3 collective-permute-start.1
  87.3 4.9 collective-permute-start
  96.0 5.4 %multiply_sine_fusion = (f32[1024,128]{1,0:T(8,128)}, f32[1024,128]{1,0:T(8,128)}, f32[1024,128]{1,0:T(8,128)}, f32[1024,128]{1,0:T(8,128)}) fusion(f32[1024]{0:T(1024)S(1)} %bitcast.96, f32[128]{0:T(128)S(1)} %multiply_power_fusion, f32[1024]{0:T(1024)S(1)} %subtract_convert_fusion), kind=kLoop, calls=%fused_computation.3 | loop fusion | flops 262144 | bytes 2105856 | tf_op jit(solution)/shard_map/sin | solution.py:387
  101.4 11.7 %project_rotate.1 = (bf16[1024,640]{1,0:T(8,128)(2,1)}, f32[1024,1024]{1,0:T(8,128)}, bf16[1024,1024]{1,0:T(8,128)(2,1)}, f32[1024,256]{1,0:T(8,128)}, bf16[2,10...) custom-call(bf16[1024,640]{1,0:T(8,128)(2,1)} %bitcast.79, ...), custom_call_target="tpu_custom_call" | custom-call | tf_op jit(solution)/shard_map/project_rotate/pallas_call | solution.py:543
  113.2 12.7 %window_attention.1 = (bf16[1024,1024]{1,0:T(8,128)(2,1)}, f32[1024,128]{1,0:T(8,128)}, f32[1024,640]{1,0:T(8,128)}, f32[1024,640]{1,0:T(8,128)}, bf16[1024,640]{1,0:T(8,128)(2,1)}) custom-call(bf16[1024,1024]{1,0:T(8,128)(2,1)} %get-tuple-element.129.q_ref, bf16[2,1024,256]{2,1,0:T(8,128)(2,1)} %get-tuple-element.130.key_ref, ...), custom_call_target="tpu_custom_call" | custom-call | tf_op jit(solution)/shard_map/window_attention/pallas_call | solution.py:577
  125.8 27.6 %all-gather.8.cloned.1.call-done = bf16[15360,256]{1,0:T(8,128)(2,1)} async-done(((bf16[480,256]{1,0:T(8,128)(2,1)}), bf16[15360,256]{1,0:T(8,128)(2,1)}) %all-gather.8.cloned.1.call-update) | async-done | bytes 7864336 | tf_op jit(solution)/shard_map/all_gather | solution.py:396
  153.4 41.4 %feed_forward.1 = (bf16[1024,640]{1,0:T(8,128)(2,1)}, bf16[1024,2048]{1,0:T(8,128)(2,1)}, bf16[1024,2048]{1,0:T(8,128)(2,1)}, bf16[1024,2048]{1,0:T(8,128)(2,1)}...) custom-call(f32[1024,640]{1,0:T(8,128)} %get-tuple-element.133.res_r, ...), custom_call_target="tpu_custom_call" | custom-call | tf_op jit(solution)/shard_map/feed_forward/pallas_call | solution.py:596
  194.9 5.5 %out_gradient.1 = bf16[8,4,80,256]{3,2,1,0:T(8,128)(2,1)} custom-call(bf16[1024,640]{1,0:T(8,128)(2,1)} %get-tuple-element.151.gffn_ref, bf16[1024,1024]{1,0:T(8,128)(2,1)} %get-tuple-element.152.hid_ref), custom_call_target="tpu_custom_call" | custom-call | tf_op jit(solution)/shard_map/out_gradient/pallas_call | solution.py:645
  200.4 16.4 %attention_gradient.1 = (bf16[1024,1024]{1,0:T(8,128)(2,1)}, bf16[2,512,512]{2,1,0:T(8,128)(2,1)}, f32[2,512,512]{2,1,0:T(8,128)}, f32[8,256]{1,0:T(8,128)}) custom-call(bf16[1024,1024]{1,0:T(8,128)(2,1)} %get-tuple-element.129.q_ref, bf16[1024,1024]{1,0:T(8,128)(2,1)} %get-tuple-element.138.gctx_ref, bf16[2,1024,256]{2,1,0:T(8,128)(2,1)} %get-tuple-element.130.key_ref, ...), custom_call_target="tpu_custom_call" | custom-call | tf_op jit(solution)/shard_map/attention_gradient/pallas_call | solution.py:657
  216.9 1.3 collective-permute-start.2
  218.2 5.5 %query_gradient.1 = bf16[8,4,160,128]{3,2,1,0:T(8,128)(2,1)} custom-call(bf16[1024,640]{1,0:T(8,128)(2,1)} %get-tuple-element.149.attn_ref, bf16[1024,1024]{1,0:T(8,128)(2,1)} %get-tuple-element.144.gq_ref), custom_call_target="tpu_custom_call" | custom-call | tf_op jit(solution)/shard_map/query_gradient/pallas_call | solution.py:679
  224.7 8.7 %input_gradient.1 = (bf16[1024,640]{1,0:T(8,128)(2,1)}, bf16[1024,512]{1,0:T(8,128)(2,1)}, f32[8,256]{1,0:T(8,128)}, f32[8,640]{1,0:T(8,128)}) custom-call(f32[2,512,512]{2,1,0:T(8,128)} %get-tuple-element.141.near_ref, bf16[2,512,512]{2,1,0:T(8,128)(2,1)} %copy-done.4, f32[1024,256]{1,0:T(8,128)} %get-tuple-element.143.kraw_ref, ...), custom_call_target="tpu_custom_call" | custom-call | tf_op jit(solution)/shard_map/input_gradient/pallas_call | solution.py:689
  233.4 3.3 key_value_gradient.1
  236.7 1.4 copy.56
  238.9 1.2 copy.57
  240.0 1.8 copy.58
  241.9 2.1 pad_maximum_fusion
  244.0 9.0 %down_gradient.1 = bf16[8,4,160,256]{3,2,1,0:T(8,128)(2,1)} custom-call(bf16[1024,640]{1,0:T(8,128)(2,1)} %get-tuple-element.155.gffn_ref, bf16[1024,2048]{1,0:T(8,128)(2,1)} %get-tuple-element.156.hid_ref), custom_call_target="tpu_custom_call" | custom-call | tf_op jit(solution)/shard_map/down_gradient/pallas_call | solution.py:625
  253.1 12.1 %gate_up_gradient.1 = bf16[8,4,320,256]{3,2,1,0:T(8,128)(2,1)} custom-call(bf16[1024,640]{1,0:T(8,128)(2,1)} %get-tuple-element.134.fin_ref, bf16[1024,2048]{1,0:T(8,128)(2,1)} %get-tuple-element.153.gg_ref, bf16[1024,2048]{1,0:T(8,128)(2,1)} %get-tuple-element.154.gu_ref), custom_call_target="tpu_custom_call" | custom-call | tf_op jit(solution)/shard_map/gate_up_gradient/pallas_call | solution.py:635
  266.0 35.6 %reduce-scatter.9.cloned.1.call-done = bf16[1,4,160,192]{3,2,1,0:T(8,128)(2,1)} async-done(((bf16[8,4,160,192]{3,2,1,0:T(8,128)(2,1)}), bf16[1,4,160,192]{3,2,1,0:T(8,128)(2,1)}) %reduce-scatter.9.cloned.1.call-update) | async-done | bytes 245776 | tf_op jit(solution)/shard_map/reduce_scatter | solution.py:400
  304.7 43.7 %reduce-scatter.21.cloned.1.call-done = bf16[1,4,160,256]{3,2,1,0:T(8,128)(2,1)} async-done(((bf16[8,4,160,256]{3,2,1,0:T(8,128)(2,1)}), bf16[1,4,160,256]{3,2,1,0:T(8,128)(2,1)}) %reduce-scatter.21.cloned.1.call-update) | async-done | bytes 327696 | tf_op jit(solution)/shard_map/reduce_scatter | solution.py:400
  348.6 39.7 %psum.7 = f32[3072]{0:T(1024)S(1)} all-reduce(f32[3072]{0:T(1024)S(1)} %constant_dynamic-update-slice_fusion), channel_id=1, replica_groups=mesh['seq'=8,'fsdp'=4] {'seq','fsdp'}, use_global_device_ids=true, to_apply=%region_13.14 | all-reduce | flops 3072 | bytes 24576 | tf_op jit(solution)/shard_map/psum | solution.py:717
  388.3 20.5 %reduce-scatter.17.cloned.1.call-done = bf16[1,4,320,256]{3,2,1,0:T(8,128)(2,1)} async-done(((bf16[8,4,320,256]{3,2,1,0:T(8,128)(2,1)}), bf16[1,4,320,256]{3,2,1,0:T(8,128)(2,1)}) %reduce-scatter.17.cloned.1.call-update) | async-done | bytes 655376 | tf_op jit(solution)/shard_map/reduce_scatter | solution.py:400
  410.1 20.4 %reduce-scatter.15.cloned.1.call-done = bf16[1,80,256]{2,1,0:T(8,128)(2,1)} async-done(((bf16[4,80,256]{2,1,0:T(8,128)(2,1)}), bf16[1,80,256]{2,1,0:T(8,128)(2,1)}) %reduce-scatter.15.cloned.1.call-update) | async-done | bytes 40976 | tf_op jit(solution)/shard_map/reduce_scatter | solution.py:401
  430.5 1.4 convert_bitcast_fusion.1
  431.9 19.0 %reduce-scatter.11.cloned.1.call-done = bf16[1,160,192]{2,1,0:T(8,128)(2,1)} async-done(((bf16[4,160,192]{2,1,0:T(8,128)(2,1)}), bf16[1,160,192]{2,1,0:T(8,128)(2,1)}) %reduce-scatter.11.cloned.1.call-update) | async-done | bytes 61456 | tf_op jit(solution)/shard_map/reduce_scatter | solution.py:401
  453.3 1.4 slice_convert_fusion.2
  454.7 16.9 %reduce-scatter.23.cloned.1.call-done = bf16[1,160,256]{2,1,0:T(8,128)(2,1)} async-done(((bf16[4,160,256]{2,1,0:T(8,128)(2,1)}), bf16[1,160,256]{2,1,0:T(8,128)(2,1)}) %reduce-scatter.23.cloned.1.call-update) | async-done | bytes 81936 | tf_op jit(solution)/shard_map/reduce_scatter | solution.py:401
  473.1 21.1 %reduce-scatter.19.cloned.1.call-done = bf16[1,320,256]{2,1,0:T(8,128)(2,1)} async-done(((bf16[4,320,256]{2,1,0:T(8,128)(2,1)}), bf16[1,320,256]{2,1,0:T(8,128)(2,1)}) %reduce-scatter.19.cloned.1.call-update) | async-done | bytes 163856 | tf_op jit(solution)/shard_map/reduce_scatter | solution.py:401
  494.2 1.7 fusion
  (115 shorter events, 22.9 us)
Async XLA Ops:
  7.2 3.8 copy-start
  7.2 68.3 %copy-start.10 = (u32[32]{0:T(128)S(1)}, u32[32]{0:T(128)}, u32[]{:S(2)}) copy-start(u32[32]{0:T(128)} %constant.67) | copy-start | bytes 388
  7.2 69.6 %copy-start.9 = (s32[2,512]{1,0:T(2,128)S(1)}, s32[2,512]{1,0:T(2,128)}, u32[]{:S(2)}) copy-start(s32[2,512]{1,0:T(2,128)} %param.19) | copy-start | bytes 12292
  7.2 80.1 %copy-start.2 = (bf16[2,512,640]{2,1,0:T(8,128)(2,1)S(1)}, bf16[2,512,640]{2,1,0:T(8,128)(2,1)}, u32[]{:S(2)}) copy-start(bf16[2,512,640]{2,1,0:T(8,128)(2,1)} %param.18) | copy-start | bytes 3932164
  7.2 68.2 %all-gather.6.cloned.1.call-start = ((), (), s32[]{:S(2)}) async-start(), calls=%async_computation.16 | async-start | bytes 4055040 | tf_op jit(solution)/shard_map/all_gather | solution.py:396
  10.9 142.6 %all-gather.8.cloned.1.call-start = ((), (), s32[]{:S(2)}) async-start(), calls=%async_computation.17 | async-start | bytes 8110080 | tf_op jit(solution)/shard_map/all_gather | solution.py:396
  11.2 82.5 %copy-start.5 = (f32[640]{0:T(1024)S(1)}, f32[640]{0:T(1024)}, u32[]{:S(2)}) copy-start(f32[640]{0:T(1024)} %param.27) | copy-start | bytes 7684
  11.2 83.1 %copy-start.6 = (f32[640]{0:T(1024)S(1)}, f32[640]{0:T(1024)}, u32[]{:S(2)}) copy-start(f32[640]{0:T(1024)} %param.28) | copy-start | bytes 7684
  11.2 83.6 %copy-start.7 = (f32[640]{0:T(1024)S(1)}, f32[640]{0:T(1024)}, u32[]{:S(2)}) copy-start(f32[640]{0:T(1024)} %param.29) | copy-start | bytes 7684
  11.2 84.2 %copy-start.8 = (f32[640]{0:T(1024)S(1)}, f32[640]{0:T(1024)}, u32[]{:S(2)}) copy-start(f32[640]{0:T(1024)} %param.30) | copy-start | bytes 7684
  75.5 189.8 %reduce-scatter.13.cloned.1.call-start = ((), (), s32[]{:S(2)}) async-start(), calls=%async_computation.10 | async-start | bytes 1474560 | tf_op jit(solution)/shard_map/reduce_scatter | solution.py:400
  86.0 10.0 %collective-permute-start.1 = (s32[2,512]{1,0:T(2,128)S(1)}, s32[2,512]{1,0:T(2,128)S(1)}, u32[]{:S(2)}, u32[]{:S(2)}) collective-permute-start(s32[2,512]{1,0:T(2,128)S(1)} %get-tuple-element.255), channel_id=1, source_target_pairs={{0,4},{4,8},{8,12},{12,16},{16,20},{20,24},{24,28},{1,5},{5,9},{9,... | collective-permute-start | bytes 12296 | tf_op jit(solution)/shard_map/ppermute | solution.py:380
  87.3 14.1 %collective-permute-start = (bf16[2,512,640]{2,1,0:T(8,128)(2,1)S(1)}, bf16[2,512,640]{2,1,0:T(8,128)(2,1)}, u32[]{:S(2)}, u32[]{:S(2)}) collective-permute-start(bf16[2,512,640]{2,1,0:T(8,128)(2,1)S(1)} %copy-done.2), channel_id=1, source_target_pairs={{0,4},{4,8},{8,12},{12,16},{16,20},{20,24},{24,28},{1,5},{5,9},{9,... | collective-permute-start | bytes 3932168 | tf_op jit(solution)/shard_map/ppermute | solution.py:380
  200.4 101.2 %reduce-scatter.9.cloned.1.call-start = ((), (), s32[]{:S(2)}) async-start(), calls=%async_computation.8 | async-start | bytes 2949120 | tf_op jit(solution)/shard_map/reduce_scatter | solution.py:400
  216.9 6.8 %collective-permute-start.2 = (bf16[2,512,512]{2,1,0:T(8,128)(2,1)}, bf16[2,512,512]{2,1,0:T(8,128)(2,1)S(1)}, u32[]{:S(2)}, u32[]{:S(2)}) collective-permute-start(bf16[2,512,512]{2,1,0:T(8,128)(2,1)} %get-tuple-element.142), channel_id=1, source_target_pairs={{4,0},{8,4},{12,8},{16,12},{20,16},{24,20},{28,24},{5,1},{9,5},{13... | collective-permute-start | bytes 3145736 | tf_op jit(solution)/shard_map/ppermute | solution.py:380
  223.7 1.0 copy-start.4
  238.8 3.0 copy-start.3
  244.0 104.4 %reduce-scatter.21.cloned.1.call-start = ((), (), s32[]{:S(2)}) async-start(), calls=%async_computation.14 | async-start | bytes 2949120 | tf_op jit(solution)/shard_map/reduce_scatter | solution.py:400
  253.0 155.9 %reduce-scatter.17.cloned.1.call-start = ((), (), s32[]{:S(2)}) async-start(), calls=%async_computation.12 | async-start | bytes 5898240 | tf_op jit(solution)/shard_map/reduce_scatter | solution.py:400
  265.2 230.6 %copy-start.1 = (bf16[512,640]{1,0:T(8,128)(2,1)S(1)}, bf16[512,640]{1,0:T(8,128)(2,1)}, u32[]{:S(2)}) copy-start(bf16[512,640]{1,0:T(8,128)(2,1)} %param.26) | copy-start | bytes 1966084
  265.2 165.3 %reduce-scatter.15.cloned.1.call-start = ((), (), s32[]{:S(2)}) async-start(), calls=%async_computation.11 | async-start | bytes 204800 | tf_op jit(solution)/shard_map/reduce_scatter | solution.py:401
  266.0 185.0 %reduce-scatter.11.cloned.1.call-start = ((), (), s32[]{:S(2)}) async-start(), calls=%async_computation.9 | async-start | bytes 409600 | tf_op jit(solution)/shard_map/reduce_scatter | solution.py:401
  301.6 170.0 %reduce-scatter.23.cloned.1.call-start = ((), (), s32[]{:S(2)}) async-start(), calls=%async_computation.15 | async-start | bytes 409600 | tf_op jit(solution)/shard_map/reduce_scatter | solution.py:401
  348.5 145.7 %reduce-scatter.19.cloned.1.call-start = ((), (), s32[]{:S(2)}) async-start(), calls=%async_computation.13 | async-start | bytes 819200 | tf_op jit(solution)/shard_map/reduce_scatter | solution.py:401
Sparse Core Ops, SparseCore 0:
  11.4 63.9 all-gather.5
  78.2 75.1 all-gather.7
  200.5 38.5 reduce-scatter.12
  244.1 57.4 reduce-scatter.8
  304.8 43.6 reduce-scatter.20
  351.7 57.1 reduce-scatter.16
  411.2 19.2 reduce-scatter.14
  432.8 18.1 reduce-scatter.10
  453.3 18.3 reduce-scatter.22
  473.7 20.3 reduce-scatter.18
